TPU v7x, 128 devices: a whole 4x4x4 slice. The times are simulated.
128 devices in a mesh: ctx: 16 (over z_hi, x, core), head: 8 (over z_lo, y).
Axes of the slice: x: 4, y: 4, z: 4 (z_hi: 2, z_lo: 2; z = z_hi * 2 + z_lo), core: 2. Of those that a mesh axis runs over, the one named last changes fastest.
Arguments:
- hidden_states: bfloat16 [16384, 4096], P('ctx'), may hold values from -6 to 6
- norm_gain: float32 [4096], replicated, may hold values from 0.5 to 2
- query_weight: bfloat16 [4096, 4096], P(None, 'head'), may hold values from -2 to 2
- key_weight: bfloat16 [4096, 1024], P(None, 'head'), may hold values from -2 to 2
- value_weight: bfloat16 [4096, 1024], P(None, 'head'), may hold values from -0.09375 to 0.09375
- output_weight: bfloat16 [4096, 4096], P('head'), may hold values from -0.09375 to 0.09375
- keep_flags: int32 [32], P('ctx'), may hold values from 0 to 1, as said below
- span_order: int32 [16], replicated, may hold values from 0 to 15, each once
Outputs:
- layer_output: bfloat16 [8192, 4096], P(('ctx', 'head'))
Inputs may be any that keep to these rules, and one draw needn't show every extreme that they name: `keep_flags`: exactly 16 of the 32 spans are kept.
All inputs are finite; a program needn't handle non-finite values.
Results may differ from a plain program's by a relative error of at most 0.02.
The roundings to bfloat16 on the way count: a program that leaves them out, or rounds other values in their place, can miss the bound.
Values may be sent and summed in bfloat16 or wider, within the bound.
A program may use at most 128 MiB of HBM per device.

v0:
```python
import math

import jax
import jax.numpy as jnp
from jax import lax
from jax.sharding import PartitionSpec as P

HEAD_DIM = 128


def rms_normed(activations, norm_gain):
    widened = activations.astype(jnp.float32)
    mean_square = jnp.mean(widened * widened, axis=-1, keepdims=True)
    return (widened * lax.rsqrt(mean_square + 1e-05) * norm_gain).astype(jnp.bfloat16)


def rotate(values, positions):
    half_width = HEAD_DIM // 2
    frequency = jnp.power(
        jnp.float32(500000.0), -2.0 * jnp.arange(half_width, dtype=jnp.float32) / HEAD_DIM
    )
    angles = positions.astype(jnp.float32)[:, None] * frequency[None, :]
    cosine = jnp.cos(angles)[:, None, :]
    sine_part = jnp.sin(angles)[:, None, :]
    shaped = values.reshape(values.shape[0], -1, HEAD_DIM)
    leading = shaped[..., :half_width]
    trailing = shaped[..., half_width:]
    turned = jnp.concatenate(
        [leading * cosine - trailing * sine_part, trailing * cosine + leading * sine_part], axis=-1
    )
    return turned.reshape(values.shape)


def project(normed, weight_matrix):
    return jnp.dot(normed, weight_matrix, preferred_element_type=jnp.float32)


def body(
    hidden_states,
    norm_gain,
    query_weight,
    key_weight,
    value_weight,
    output_weight,
    keep_flags,
    span_order,
):
    devices_ctx = lax.axis_size("ctx")
    my_index = lax.axis_index("ctx")
    spans_here = keep_flags.shape[0]
    span_rows = hidden_states.shape[0] // spans_here
    piece_rows = span_rows // devices_ctx
    kept_total = span_order.shape[0]
    rows_here = kept_total * piece_rows
    all_flags = lax.all_gather(keep_flags, "ctx", axis=0, tiled=True)
    span_count = all_flags.shape[0]
    global_rank = jnp.cumsum(all_flags) - 1
    slot_range = jnp.arange(kept_total, dtype=jnp.int32)
    span_range = jnp.arange(span_count, dtype=jnp.int32)
    selected = (all_flags[None, :] == 1) & (global_rank[None, :] == slot_range[:, None])
    span_ids = jnp.sum(jnp.where(selected, span_range[None, :], 0), axis=1)
    shifts = span_order % devices_ctx

    def lookup(lookup_table, indices):
        return jnp.sum(
            jnp.where(indices[:, None] == slot_range[None, :], lookup_table[None, :], 0), axis=1
        )

    def positions_of(global_rows):
        owner_device = global_rows // rows_here
        within = global_rows % rows_here // piece_rows
        return (
            lookup(span_ids, within) * span_rows
            + (owner_device - lookup(shifts, within)) % devices_ctx * piece_rows
            + global_rows % piece_rows
        )

    my_positions = positions_of(my_index * rows_here + jnp.arange(rows_here, dtype=jnp.int32))
    local_rank = jnp.cumsum(keep_flags) - 1
    local_count = jnp.sum(keep_flags)
    capacity_slots = jnp.arange(spans_here, dtype=jnp.int32)
    picked = (keep_flags[None, :] == 1) & (local_rank[None, :] == capacity_slots[:, None])
    slot_span = jnp.sum(jnp.where(picked, capacity_slots[None, :], 0), axis=1)
    first_rank = jnp.sum(jnp.where(span_range < my_index * spans_here, all_flags, 0))
    slot_shift = lookup(shifts, first_rank + capacity_slots)
    slot_valid = capacity_slots < local_count
    targets = jnp.arange(devices_ctx, dtype=jnp.int32)
    piece_index = (targets[:, None] - slot_shift[None, :]) % devices_ctx
    source_rows = (
        slot_span[None, :, None] * span_rows
        + piece_index[:, :, None] * piece_rows
        + jnp.arange(piece_rows, dtype=jnp.int32)[None, None, :]
    )
    source_counts = jnp.sum(all_flags.reshape(devices_ctx, spans_here), axis=1)
    source_starts = jnp.cumsum(source_counts) - source_counts
    owner_of = span_ids // spans_here
    start_of = jnp.sum(
        jnp.where(owner_of[:, None] == targets[None, :], source_starts[None, :], 0), axis=1
    )
    arrival = owner_of * spans_here + slot_range - start_of
    query_cols = query_weight.shape[1]
    key_cols = key_weight.shape[1]
    normed = rms_normed(hidden_states, norm_gain)
    raw_positions = my_index * spans_here * span_rows + jnp.arange(
        hidden_states.shape[0], dtype=jnp.int32
    )
    query_raw = rotate(project(normed, query_weight), raw_positions).astype(jnp.bfloat16)
    key_raw = rotate(project(normed, key_weight), raw_positions).astype(jnp.bfloat16)
    value_raw = project(normed, value_weight).astype(jnp.bfloat16)
    joined = jnp.concatenate([query_raw, key_raw, value_raw], axis=1)
    width_cols = joined.shape[1]
    gathered = joined[source_rows.reshape(-1)].reshape(
        devices_ctx, spans_here, piece_rows, width_cols
    )
    received = lax.all_to_all(
        jnp.where(slot_valid[None, :, None, None], gathered, jnp.zeros_like(gathered)),
        "ctx",
        split_axis=0,
        concat_axis=0,
        tiled=True,
    )
    width_cols = received.shape[3]
    flattened = received.reshape(devices_ctx * spans_here, piece_rows, width_cols)
    arrived = flattened[arrival].reshape(rows_here, width_cols)
    query_states = arrived[:, :query_cols]
    key_states = arrived[:, query_cols : query_cols + key_cols]
    value_states = arrived[:, query_cols + key_cols :]
    kv_local = key_cols // HEAD_DIM
    group_size = query_cols // HEAD_DIM // kv_local
    grouped = query_states.reshape(rows_here, kv_local, group_size, HEAD_DIM)
    score_scale = 1.0 / math.sqrt(HEAD_DIM)
    initial = (
        jnp.full((kv_local, group_size, rows_here), -1e30, jnp.float32),
        jnp.zeros((kv_local, group_size, rows_here), jnp.float32),
        jnp.zeros((kv_local, group_size, rows_here, HEAD_DIM), jnp.float32),
    )
    key_piece = lax.all_gather(key_states, "ctx", axis=0, tiled=True)
    value_piece = lax.all_gather(value_states, "ctx", axis=0, tiled=True)
    piece_length = key_piece.shape[0]
    block_rows = math.gcd(piece_length, 512)
    key_positions = positions_of(jnp.arange(piece_length, dtype=jnp.int32))

    def advance(block_index, state):
        running, denominator, accumulated = state
        offset = block_index * block_rows
        key_block = lax.dynamic_slice_in_dim(key_piece, offset, block_rows, 0).reshape(
            block_rows, kv_local, HEAD_DIM
        )
        value_block = lax.dynamic_slice_in_dim(value_piece, offset, block_rows, 0).reshape(
            block_rows, kv_local, HEAD_DIM
        )
        block_positions = lax.dynamic_slice_in_dim(key_positions, offset, block_rows, 0)
        scores = (
            jnp.einsum("qkgd,nkd->kgqn", grouped, key_block, preferred_element_type=jnp.float32)
            * score_scale
        )
        allowed = block_positions[None, None, None, :] <= my_positions[None, None, :, None]
        scores = jnp.where(allowed, scores, -1e30)
        new_peak = jnp.maximum(running, jnp.max(scores, axis=3))
        rescale = jnp.exp(running - new_peak)
        expo = jnp.where(allowed, jnp.exp(scores - new_peak[..., None]), 0.0)
        denominator = denominator * rescale + jnp.sum(expo, axis=3)
        accumulated = accumulated * rescale[..., None] + jnp.einsum(
            "kgqn,nkd->kgqd",
            expo.astype(jnp.bfloat16),
            value_block,
            preferred_element_type=jnp.float32,
        )
        return (new_peak, denominator, accumulated)

    running, denominator, accumulated = lax.fori_loop(
        0, piece_length // block_rows, advance, initial
    )
    attended = (
        (accumulated / denominator[..., None])
        .transpose(2, 0, 1, 3)
        .reshape(rows_here, query_cols)
        .astype(jnp.bfloat16)
    )
    return lax.psum_scatter(
        jnp.dot(attended, output_weight, preferred_element_type=jnp.float32).astype(jnp.bfloat16),
        "head",
        scatter_dimension=0,
        tiled=True,
    )


def solution(mesh):
    return jax.shard_map(
        body,
        mesh=mesh,
        in_specs=(
            P("ctx", None),
            P(),
            P(None, "head"),
            P(None, "head"),
            P(None, "head"),
            P("head", None),
            P("ctx"),
            P(),
        ),
        out_specs=P(("ctx", "head"), None),
        check_vma=False,
    )
```

profile of v0, /device:TPU:32, one launch (start us, length us, event | category | flops | bytes accessed | tf_op | source)
XLA Modules:
  0.0 418.4 jit_solution(15126154366941655470)
XLA Ops:
  6.6 5.2 %fusion.25 = f32[1024]{0:T(1024)S(1)} fusion(bf16[1024,4096]{1,0:T(8,128)(2,1)} %param.10), kind=kLoop, calls=%fused_computation.32 | loop fusion | flops 12581888 | bytes 8392704 | tf_op jit(solution)/shard_map/reduce_sum | solution.py:13
  12.8 10.3 %fusion.27 = bf16[1024,4096]{1,0:T(8,128)(2,1)} fusion(bf16[1024,4096]{1,0:T(8,128)(2,1)} %param.10, f32[4096]{0:T(1024)S(1)} %copy-done.5, f32[1024]{0:T(1024)S(1)} %add_rsqrt_fusion), kind=kLoop, calls=%fused_computation.34 | loop fusion | flops 16777216 | bytes 16797696 | tf_op jit(solution)/shard_map/convert_element_type | solution.py:14
  23.1 8.2 %fusion.75 = f32[1024,512]{0,1:T(8,128)S(1)} fusion(bf16[1024,4096]{1,0:T(8,128)(2,1)} %fusion.27, bf16[4096,512]{1,0:T(8,128)(2,1)} %param.12), kind=kOutput, calls=%fused_computation.172 | convolution fusion | flops 4294967296 | bytes 14680064 | tf_op jit(solution)/shard_map/dot_general | solution.py:35
  33.2 6.4 %convolution_bitcast_fusion = f32[1024,1,128]{0,2,1:T(8,128)S(1)} fusion(bf16[1024,4096]{1,0:T(8,128)(2,1)} %fusion.27, bf16[4096,128]{1,0:T(8,128)(2,1)S(1)} %copy-done), kind=kOutput, calls=%fused_computation.38 | convolution fusion | flops 1073741824 | bytes 9961472 | tf_op jit(solution)/shard_map/dot_general | solution.py:35
  41.0 6.3 %convolution_convert_fusion.1 = bf16[1024,128]{0,1:T(8,128)(2,1)S(1)} fusion(bf16[1024,4096]{1,0:T(8,128)(2,1)} %fusion.27, bf16[4096,128]{1,0:T(8,128)(2,1)S(1)} %copy-done.4), kind=kOutput, calls=%fused_computation.39 | convolution fusion | flops 1073872896 | bytes 9699328 | tf_op jit(solution)/shard_map/dot_general | solution.py:35
  49.7 13.8 %all-reduce = s32[32]{0:T(128)S(1)} all-reduce(s32[32]{0:T(128)S(1)} %dynamic-update-slice), channel_id=1, replica_groups=mesh['ctx'=16,'head'=8] {'ctx'}, use_global_device_ids=true, to_apply=%add | all-reduce | flops 32 | bytes 256
  67.6 5.2 %gather_fusion = bf16[1024,768]{1,0:T(8,128)(2,1)} fusion(bf16[1024,768]{1,0:T(8,128)(2,1)S(1)} %pad_maximum_fusion, s32[1024]{0:T(1024)S(1)} %broadcast_clamp_fusion), kind=kCustom, calls=%fused_computation | custom fusion | bytes 3149824 | tf_op jit(solution)/shard_map/gather | solution.py:112
  80.4 22.4 %all-to-all-done = bf16[16,2,32,768]{3,2,1,0:T(8,128)(2,1)S(1)} async-done(((bf16[16,2,32,768]{3,2,1,0:T(8,128)(2,1)}), bf16[16,2,32,768]{3,2,1,0:T(8,128)(2,1)S(1)}, u32[]{:S(2)}, u32[]{:S(2)}) %all-to-all-start) | async-done | bytes 1572896 | tf_op jit(solution)/shard_map/all_to_all | solution.py:115
  106.0 44.4 %all-gather.3.cloned.1.call-done = bf16[8192,128]{1,0:T(8,128)(2,1)} async-done(((bf16[512,128]{1,0:T(8,128)(2,1)}), bf16[8192,128]{1,0:T(8,128)(2,1)}) %all-gather.3.cloned.1.call-update) | async-done | bytes 2097168 | tf_op jit(solution)/shard_map/all_gather | solution.py:137
  150.4 49.6 %all-gather.5.cloned.1.call-done = bf16[8192,128]{1,0:T(8,128)(2,1)} async-done(((bf16[512,128]{1,0:T(8,128)(2,1)}), bf16[8192,128]{1,0:T(8,128)(2,1)}) %all-gather.5.cloned.1.call-update) | async-done | bytes 2097168 | tf_op jit(solution)/shard_map/all_gather | solution.py:138
  200.0 151.9 %while.18 = (s32[]{:T(128)}, f32[1,4,512]{2,1,0:T(4,128)S(1)}, f32[1,4,512]{2,1,0:T(4,128)S(1)}, f32[1,4,512,128]{3,2,1,0:T(8,128)}, s32[8192]{0:T(1024)S(1)}, /...) while((s32[]{:T(128)}, f32[1,4,512]{2,1,0:T(4,128)S(1)}, ...), condition=%wide.region_18.19_spmd.clone, body=%wide.region_15.18_spmd.clone.sunk | while | flops 551563264 | bytes 41820436 | solution.py:171
  204.0 4.3 %fusion.95 = f32[1,4,512,128]{3,2,1,0:T(8,128)S(1)} fusion(f32[512,512,4]{1,0,2:T(8,128)} %get-tuple-element.314, f32[4,512]{1,0:T(4,128)S(1)} %bitcast.121, pred[512,512]{0,1:T(8,128)(4,1)S(1)} %broadcast_compare_fusion.4, f32[1,4,512,128]{3,2,1,0:T(8,128)S(1)} %copy-done.2, f32[4,512]{1,0:T(4,128)S(1)} %get-tuple-element.315, pred[]{:T(512)S(6)} %compare.49, ...), kind=kOutput, calls=%fused_computation.11.clone.1 | convolution fusion | flops 274464768 | bytes 6701061 | tf_op jit(solution)/shard_map/while/body/eval_jaxpr/kgqn,nkd->kgqd/dot_general | solution.py:163
  213.5 4.3 %fusion.95 = f32[1,4,512,128]{3,2,1,0:T(8,128)S(1)} fusion(f32[512,512,4]{1,0,2:T(8,128)} %get-tuple-element.314, f32[4,512]{1,0:T(4,128)S(1)} %bitcast.121, pred[512,512]{0,1:T(8,128)(4,1)S(1)} %broadcast_compare_fusion.4, f32[1,4,512,128]{3,2,1,0:T(8,128)S(1)} %copy-done.2, f32[4,512]{1,0:T(4,128)S(1)} %get-tuple-element.315, pred[]{:T(512)S(6)} %compare.49, ...), kind=kOutput, calls=%fused_computation.11.clone.1 | convolution fusion | flops 274464768 | bytes 6701061 | tf_op jit(solution)/shard_map/while/body/eval_jaxpr/kgqn,nkd->kgqd/dot_general | solution.py:163
  223.0 4.3 %fusion.95 = f32[1,4,512,128]{3,2,1,0:T(8,128)S(1)} fusion(f32[512,512,4]{1,0,2:T(8,128)} %get-tuple-element.314, f32[4,512]{1,0:T(4,128)S(1)} %bitcast.121, pred[512,512]{0,1:T(8,128)(4,1)S(1)} %broadcast_compare_fusion.4, f32[1,4,512,128]{3,2,1,0:T(8,128)S(1)} %copy-done.2, f32[4,512]{1,0:T(4,128)S(1)} %get-tuple-element.315, pred[]{:T(512)S(6)} %compare.49, ...), kind=kOutput, calls=%fused_computation.11.clone.1 | convolution fusion | flops 274464768 | bytes 6701061 | tf_op jit(solution)/shard_map/while/body/eval_jaxpr/kgqn,nkd->kgqd/dot_general | solution.py:163
  232.5 4.3 %fusion.95 = f32[1,4,512,128]{3,2,1,0:T(8,128)S(1)} fusion(f32[512,512,4]{1,0,2:T(8,128)} %get-tuple-element.314, f32[4,512]{1,0:T(4,128)S(1)} %bitcast.121, pred[512,512]{0,1:T(8,128)(4,1)S(1)} %broadcast_compare_fusion.4, f32[1,4,512,128]{3,2,1,0:T(8,128)S(1)} %copy-done.2, f32[4,512]{1,0:T(4,128)S(1)} %get-tuple-element.315, pred[]{:T(512)S(6)} %compare.49, ...), kind=kOutput, calls=%fused_computation.11.clone.1 | convolution fusion | flops 274464768 | bytes 6701061 | tf_op jit(solution)/shard_map/while/body/eval_jaxpr/kgqn,nkd->kgqd/dot_general | solution.py:163
  242.0 4.3 %fusion.95 = f32[1,4,512,128]{3,2,1,0:T(8,128)S(1)} fusion(f32[512,512,4]{1,0,2:T(8,128)} %get-tuple-element.314, f32[4,512]{1,0:T(4,128)S(1)} %bitcast.121, pred[512,512]{0,1:T(8,128)(4,1)S(1)} %broadcast_compare_fusion.4, f32[1,4,512,128]{3,2,1,0:T(8,128)S(1)} %copy-done.2, f32[4,512]{1,0:T(4,128)S(1)} %get-tuple-element.315, pred[]{:T(512)S(6)} %compare.49, ...), kind=kOutput, calls=%fused_computation.11.clone.1 | convolution fusion | flops 274464768 | bytes 6701061 | tf_op jit(solution)/shard_map/while/body/eval_jaxpr/kgqn,nkd->kgqd/dot_general | solution.py:163
  251.5 4.3 %fusion.95 = f32[1,4,512,128]{3,2,1,0:T(8,128)S(1)} fusion(f32[512,512,4]{1,0,2:T(8,128)} %get-tuple-element.314, f32[4,512]{1,0:T(4,128)S(1)} %bitcast.121, pred[512,512]{0,1:T(8,128)(4,1)S(1)} %broadcast_compare_fusion.4, f32[1,4,512,128]{3,2,1,0:T(8,128)S(1)} %copy-done.2, f32[4,512]{1,0:T(4,128)S(1)} %get-tuple-element.315, pred[]{:T(512)S(6)} %compare.49, ...), kind=kOutput, calls=%fused_computation.11.clone.1 | convolution fusion | flops 274464768 | bytes 6701061 | tf_op jit(solution)/shard_map/while/body/eval_jaxpr/kgqn,nkd->kgqd/dot_general | solution.py:163
  261.0 4.3 %fusion.95 = f32[1,4,512,128]{3,2,1,0:T(8,128)S(1)} fusion(f32[512,512,4]{1,0,2:T(8,128)} %get-tuple-element.314, f32[4,512]{1,0:T(4,128)S(1)} %bitcast.121, pred[512,512]{0,1:T(8,128)(4,1)S(1)} %broadcast_compare_fusion.4, f32[1,4,512,128]{3,2,1,0:T(8,128)S(1)} %copy-done.2, f32[4,512]{1,0:T(4,128)S(1)} %get-tuple-element.315, pred[]{:T(512)S(6)} %compare.49, ...), kind=kOutput, calls=%fused_computation.11.clone.1 | convolution fusion | flops 274464768 | bytes 6701061 | tf_op jit(solution)/shard_map/while/body/eval_jaxpr/kgqn,nkd->kgqd/dot_general | solution.py:163
  270.5 4.3 %fusion.95 = f32[1,4,512,128]{3,2,1,0:T(8,128)S(1)} fusion(f32[512,512,4]{1,0,2:T(8,128)} %get-tuple-element.314, f32[4,512]{1,0:T(4,128)S(1)} %bitcast.121, pred[512,512]{0,1:T(8,128)(4,1)S(1)} %broadcast_compare_fusion.4, f32[1,4,512,128]{3,2,1,0:T(8,128)S(1)} %copy-done.2, f32[4,512]{1,0:T(4,128)S(1)} %get-tuple-element.315, pred[]{:T(512)S(6)} %compare.49, ...), kind=kOutput, calls=%fused_computation.11.clone.1 | convolution fusion | flops 274464768 | bytes 6701061 | tf_op jit(solution)/shard_map/while/body/eval_jaxpr/kgqn,nkd->kgqd/dot_general | solution.py:163
  280.0 4.3 %fusion.95 = f32[1,4,512,128]{3,2,1,0:T(8,128)S(1)} fusion(f32[512,512,4]{1,0,2:T(8,128)} %get-tuple-element.314, f32[4,512]{1,0:T(4,128)S(1)} %bitcast.121, pred[512,512]{0,1:T(8,128)(4,1)S(1)} %broadcast_compare_fusion.4, f32[1,4,512,128]{3,2,1,0:T(8,128)S(1)} %copy-done.2, f32[4,512]{1,0:T(4,128)S(1)} %get-tuple-element.315, pred[]{:T(512)S(6)} %compare.49, ...), kind=kOutput, calls=%fused_computation.11.clone.1 | convolution fusion | flops 274464768 | bytes 6701061 | tf_op jit(solution)/shard_map/while/body/eval_jaxpr/kgqn,nkd->kgqd/dot_general | solution.py:163
  299.0 4.3 %fusion.95 = f32[1,4,512,128]{3,2,1,0:T(8,128)S(1)} fusion(f32[512,512,4]{1,0,2:T(8,128)} %get-tuple-element.314, f32[4,512]{1,0:T(4,128)S(1)} %bitcast.121, pred[512,512]{0,1:T(8,128)(4,1)S(1)} %broadcast_compare_fusion.4, f32[1,4,512,128]{3,2,1,0:T(8,128)S(1)} %copy-done.2, f32[4,512]{1,0:T(4,128)S(1)} %get-tuple-element.315, pred[]{:T(512)S(6)} %compare.49, ...), kind=kOutput, calls=%fused_computation.11.clone.1 | convolution fusion | flops 274464768 | bytes 6701061 | tf_op jit(solution)/shard_map/while/body/eval_jaxpr/kgqn,nkd->kgqd/dot_general | solution.py:163
  327.4 4.3 %fusion.95 = f32[1,4,512,128]{3,2,1,0:T(8,128)S(1)} fusion(f32[512,512,4]{1,0,2:T(8,128)} %get-tuple-element.314, f32[4,512]{1,0:T(4,128)S(1)} %bitcast.121, pred[512,512]{0,1:T(8,128)(4,1)S(1)} %broadcast_compare_fusion.4, f32[1,4,512,128]{3,2,1,0:T(8,128)S(1)} %copy-done.2, f32[4,512]{1,0:T(4,128)S(1)} %get-tuple-element.315, pred[]{:T(512)S(6)} %compare.49, ...), kind=kOutput, calls=%fused_computation.11.clone.1 | convolution fusion | flops 274464768 | bytes 6701061 | tf_op jit(solution)/shard_map/while/body/eval_jaxpr/kgqn,nkd->kgqd/dot_general | solution.py:163
  353.6 6.5 %convolution_convert_fusion = bf16[512,4096]{1,0:T(8,128)(2,1)} fusion(bf16[512,512]{0,1:T(8,128)(2,1)S(1)} %bitcast.125, bf16[512,4096]{1,0:T(8,128)(2,1)} %param.15), kind=kOutput, calls=%fused_computation.35 | convolution fusion | flops 2149580800 | bytes 8912896 | tf_op jit(solution)/shard_map/dot_general | solution.py:181
  360.1 51.8 %reduce-scatter.2.cloned.1.call-done = bf16[64,4096]{1,0:T(8,128)(2,1)} async-done(((bf16[512,4096]{1,0:T(8,128)(2,1)}), bf16[64,4096]{1,0:T(8,128)(2,1)}) %reduce-scatter.2.cloned.1.call-update) | async-done | bytes 524304 | tf_op jit(solution)/shard_map/reduce_scatter | solution.py:180
  (295 shorter events, 125.1 us)
Async XLA Ops:
  6.5 26.7 %copy-start = (bf16[4096,128]{1,0:T(8,128)(2,1)S(1)}, bf16[4096,128]{1,0:T(8,128)(2,1)}, u32[]{:S(2)}) copy-start(bf16[4096,128]{1,0:T(8,128)(2,1)} %param.13) | copy-start | bytes 3145732
  6.6 6.2 %copy-start.5 = (f32[4096]{0:T(1024)S(1)}, f32[4096]{0:T(1024)}, u32[]{:S(2)}) copy-start(f32[4096]{0:T(1024)} %param.11) | copy-start | bytes 49156
  33.2 7.7 %copy-start.4 = (bf16[4096,128]{1,0:T(8,128)(2,1)S(1)}, bf16[4096,128]{1,0:T(8,128)(2,1)}, u32[]{:S(2)}) copy-start(bf16[4096,128]{1,0:T(8,128)(2,1)} %param.14) | copy-start | bytes 3145732
  41.0 6.5 %copy-start.7 = (s32[2]{0:T(128)S(1)}, s32[2]{0:T(128)}, u32[]{:S(2)}) copy-start(s32[2]{0:T(128)} %param.16) | copy-start | bytes 28
  41.0 7.2 %copy-start.8 = (u32[128]{0:T(128)S(1)}, u32[128]{0:T(128)}, u32[]{:S(2)}) copy-start(u32[128]{0:T(128)} %constant.235) | copy-start | bytes 1540
  41.0 23.8 %copy-start.6 = (s32[16]{0:T(128)S(1)}, s32[16]{0:T(128)}, u32[]{:S(2)}) copy-start(s32[16]{0:T(128)} %param.17) | copy-start | bytes 196
  75.5 27.3 %all-to-all-start = ((bf16[16,2,32,768]{3,2,1,0:T(8,128)(2,1)}), bf16[16,2,32,768]{3,2,1,0:T(8,128)(2,1)S(1)}, u32[]{:S(2)}, u32[]{:S(2)}) async-start(bf16[16,2,32,768]{3,2,1,0:T(8,128)(2,1)} %broadcast_select_fusion), calls=%async_computation | async-start | bytes 3145728 | tf_op jit(solution)/shard_map/all_to_all | solution.py:115
  79.2 71.2 %all-gather.3.cloned.1.call-start = ((), (), s32[]{:S(2)}) async-start(), calls=%async_computation.2 | async-start | bytes 2228224 | tf_op jit(solution)/shard_map/all_gather | solution.py:137
  104.1 95.8 %all-gather.5.cloned.1.call-start = ((), (), s32[]{:S(2)}) async-start(), calls=%async_computation.3 | async-start | bytes 2228224 | tf_op jit(solution)/shard_map/all_gather | solution.py:138
  104.9 307.0 %reduce-scatter.2.cloned.1.call-start = ((), (), s32[]{:S(2)}) async-start(), calls=%async_computation.4 | async-start | bytes 4718592 | tf_op jit(solution)/shard_map/reduce_scatter | solution.py:180
  204.0 4.3 %copy-start.1 = (f32[512,512,4]{1,0,2:T(8,128)S(1)}, f32[512,512,4]{1,0,2:T(8,128)}, u32[]{:S(2)}) copy-start(f32[512,512,4]{1,0,2:T(8,128)} %get-tuple-element.314) | copy-start | bytes 12582916 | tf_op jit(solution)/shard_map/while
  213.5 4.3 %copy-start.1 = (f32[512,512,4]{1,0,2:T(8,128)S(1)}, f32[512,512,4]{1,0,2:T(8,128)}, u32[]{:S(2)}) copy-start(f32[512,512,4]{1,0,2:T(8,128)} %get-tuple-element.314) | copy-start | bytes 12582916 | tf_op jit(solution)/shard_map/while
  223.0 4.3 %copy-start.1 = (f32[512,512,4]{1,0,2:T(8,128)S(1)}, f32[512,512,4]{1,0,2:T(8,128)}, u32[]{:S(2)}) copy-start(f32[512,512,4]{1,0,2:T(8,128)} %get-tuple-element.314) | copy-start | bytes 12582916 | tf_op jit(solution)/shard_map/while
  232.5 4.3 %copy-start.1 = (f32[512,512,4]{1,0,2:T(8,128)S(1)}, f32[512,512,4]{1,0,2:T(8,128)}, u32[]{:S(2)}) copy-start(f32[512,512,4]{1,0,2:T(8,128)} %get-tuple-element.314) | copy-start | bytes 12582916 | tf_op jit(solution)/shard_map/while
  242.0 4.3 %copy-start.1 = (f32[512,512,4]{1,0,2:T(8,128)S(1)}, f32[512,512,4]{1,0,2:T(8,128)}, u32[]{:S(2)}) copy-start(f32[512,512,4]{1,0,2:T(8,128)} %get-tuple-element.314) | copy-start | bytes 12582916 | tf_op jit(solution)/shard_map/while
  251.5 4.3 %copy-start.1 = (f32[512,512,4]{1,0,2:T(8,128)S(1)}, f32[512,512,4]{1,0,2:T(8,128)}, u32[]{:S(2)}) copy-start(f32[512,512,4]{1,0,2:T(8,128)} %get-tuple-element.314) | copy-start | bytes 12582916 | tf_op jit(solution)/shard_map/while
  261.0 4.3 %copy-start.1 = (f32[512,512,4]{1,0,2:T(8,128)S(1)}, f32[512,512,4]{1,0,2:T(8,128)}, u32[]{:S(2)}) copy-start(f32[512,512,4]{1,0,2:T(8,128)} %get-tuple-element.314) | copy-start | bytes 12582916 | tf_op jit(solution)/shard_map/while
  270.5 4.3 %copy-start.1 = (f32[512,512,4]{1,0,2:T(8,128)S(1)}, f32[512,512,4]{1,0,2:T(8,128)}, u32[]{:S(2)}) copy-start(f32[512,512,4]{1,0,2:T(8,128)} %get-tuple-element.314) | copy-start | bytes 12582916 | tf_op jit(solution)/shard_map/while
  280.0 4.3 %copy-start.1 = (f32[512,512,4]{1,0,2:T(8,128)S(1)}, f32[512,512,4]{1,0,2:T(8,128)}, u32[]{:S(2)}) copy-start(f32[512,512,4]{1,0,2:T(8,128)} %get-tuple-element.314) | copy-start | bytes 12582916 | tf_op jit(solution)/shard_map/while
  289.5 4.3 %copy-start.1 = (f32[512,512,4]{1,0,2:T(8,128)S(1)}, f32[512,512,4]{1,0,2:T(8,128)}, u32[]{:S(2)}) copy-start(f32[512,512,4]{1,0,2:T(8,128)} %get-tuple-element.314) | copy-start | bytes 12582916 | tf_op jit(solution)/shard_map/while
  298.9 4.3 %copy-start.1 = (f32[512,512,4]{1,0,2:T(8,128)S(1)}, f32[512,512,4]{1,0,2:T(8,128)}, u32[]{:S(2)}) copy-start(f32[512,512,4]{1,0,2:T(8,128)} %get-tuple-element.314) | copy-start | bytes 12582916 | tf_op jit(solution)/shard_map/while
  317.9 4.3 %copy-start.1 = (f32[512,512,4]{1,0,2:T(8,128)S(1)}, f32[512,512,4]{1,0,2:T(8,128)}, u32[]{:S(2)}) copy-start(f32[512,512,4]{1,0,2:T(8,128)} %get-tuple-element.314) | copy-start | bytes 12582916 | tf_op jit(solution)/shard_map/while
  327.4 4.3 %copy-start.1 = (f32[512,512,4]{1,0,2:T(8,128)S(1)}, f32[512,512,4]{1,0,2:T(8,128)}, u32[]{:S(2)}) copy-start(f32[512,512,4]{1,0,2:T(8,128)} %get-tuple-element.314) | copy-start | bytes 12582916 | tf_op jit(solution)/shard_map/while
  346.4 4.3 %copy-start.1 = (f32[512,512,4]{1,0,2:T(8,128)S(1)}, f32[512,512,4]{1,0,2:T(8,128)}, u32[]{:S(2)}) copy-start(f32[512,512,4]{1,0,2:T(8,128)} %get-tuple-element.314) | copy-start | bytes 12582916 | tf_op jit(solution)/shard_map/while
  (34 other events, 90.7 us)
Sparse Core Ops, SparseCore 0:
  104.3 46.0 all-gather.2
  152.8 47.0 all-gather.4
  360.2 51.6 reduce-scatter.1
where the time goes:
time: 421 us; the launch traced here: 418 us
  waiting for transfers between devices  169 us (40%)
  matrix products  156 us (37%)
  other arithmetic  47.6 us (11%)
  between operations  14.1 us (3%)
  blocking collectives  13.8 us (3%)
  local copies, waits for them, and re-layouts  13 us (3%)
    dot_general x16, matrix products, advance(): jnp.einsum('kgqn,nkd->kgqd', expo.astype(jnp.bfloat16), value_block, pref...  69 us
    dot_general x16, matrix products, advance(): jnp.einsum('qkgd,nkd->kgqn', grouped, key_block, preferred_element_type=j...  59.1 us
    reduce_scatter x1, waiting for transfers between devices, body(): lax.psum_scatter(jnp.dot(attended, output_weight, preferred_element_type=...  51.8 us
    all_gather x1, waiting for transfers between devices, body(): value_piece = lax.all_gather(value_states, 'ctx', axis=0, tiled=True)  49.6 us
    all_gather x1, waiting for transfers between devices, body(): key_piece = lax.all_gather(key_states, 'ctx', axis=0, tiled=True)  44.4 us
    all_to_all x1, waiting for transfers between devices, body(): lax.all_to_all(jnp.where(slot_valid[None, :, None, None], gathered, jnp.z...  22.4 us
    dot_general x3, matrix products, project(): return jnp.dot(normed, weight_matrix, preferred_element_type=jnp.float32)  20.9 us
    reduce_sum x16, other arithmetic, advance(): denominator = denominator * rescale + jnp.sum(expo, axis=3)  16.8 us
  transfers between devices with their start and end apart: 4, of which 4 were waited for; matrix products, arithmetic and copies ran while one was open for 0% of the time, Pallas kernels for 0%

commit v1 on v0

v1 whole, which is shorter than its diff:
```python
import functools
import math

import jax
import jax.numpy as jnp
import numpy as np
from jax import lax
from jax.experimental import pallas as pl
from jax.experimental.pallas import tpu as pltpu
from jax.sharding import PartitionSpec as P

MESH = pl.DeviceIdType.MESH
HEAD_DIM = 128
PIECE = 32
KEPT = 16
SPAN = 512
N_CTX = 16
LOG2E = math.log2(math.e)
F32 = jnp.float32
BF16 = jnp.bfloat16


def rope_tables():
    frequency = 500000.0 ** (-2.0 * np.arange(64, dtype=np.float64) / HEAD_DIM)
    frequency = np.concatenate([frequency, frequency])[None, :]
    sign = np.concatenate([-np.ones(64), np.ones(64)])[None, :]
    pieces = np.arange(N_CTX * 2 * SPAN // PIECE, dtype=np.float64)[:, None] * PIECE * frequency
    rows = np.arange(PIECE, dtype=np.float64)[:, None] * frequency
    base = np.stack([np.cos(pieces), np.sin(pieces)]).reshape(2, N_CTX, 32, 1, HEAD_DIM)
    inner = np.stack([np.cos(rows), np.sin(rows), np.cos(rows) * sign, np.sin(rows) * sign])
    return base.transpose(1, 2, 0, 3, 4).astype(np.float32), inner.astype(np.float32)


def kernel(
    hidden_hbm, gain_ref, wq_hbm, wk_hbm, wv_hbm, wo_hbm, flags_ref, order_ref, base_hbm, inner_ref,
    out_ref,
    hidden, wqkv, wo, wo_a, wo_b, base, normed, flag_src, flag_all, flag_sm, stage, recv,
    queries, kv, acc, peak, att, att_a, att_b, part_a, part_b, got_a, got_b, mine, zsend, zgot,
    load_sem, flag_send, flag_recv, a2a_send, a2a_recv, kv_send, kv_recv, w_send, w_recv, wc_send, wc_recv,
    att_send, att_recv, part_send, part_recv, z_send, z_recv, local_sem,
):
    me = lax.axis_index("ctx")
    head = lax.axis_index("head")
    zh, x, core = me // 8, (me // 2) % 4, me % 2
    zl, y = head // 4, head % 4
    pa = y + 1 - 2 * (y % 2)
    pb = 3 - y

    def ctx_at(dz, dx, dc):
        return ((zh + dz) % 2) * 8 + ((x + dx) % 4) * 2 + (core + dc) % 2

    def send(src, dst, ssem, rsem, ctx=None, hd=None):
        copy = pltpu.make_async_remote_copy(
            src_ref=src, dst_ref=dst, send_sem=ssem, recv_sem=rsem,
            device_id=(me if ctx is None else ctx, head if hd is None else hd),
            device_id_type=MESH,
        )
        copy.start()
        return copy

    def await_recv(dst, rsem):
        pltpu.make_async_remote_copy(
            src_ref=dst, dst_ref=dst, send_sem=rsem, recv_sem=rsem,
            device_id=(me, head), device_id_type=MESH,
        ).wait_recv()

    sends = []

    loads = []

    def load(src, dst):
        copy = pltpu.make_async_copy(src, dst, load_sem.at[len(loads)])
        copy.start()
        loads.append(copy)
        return copy

    load_base = load(base_hbm.at[me], base)
    load_hidden = load(hidden_hbm, hidden)
    load_q = load(wq_hbm, wqkv.at[:, pl.ds(0, 512)])
    load_k = load(wk_hbm, wqkv.at[:, pl.ds(512, 128)])
    load_v = load(wv_hbm, wqkv.at[:, pl.ds(640, 128)])
    load_o = load(wo_hbm, wo)

    barrier = pltpu.get_barrier_semaphore()
    for i in range(1, N_CTX):
        pl.semaphore_signal(barrier, inc=1, device_id=((me + i) % N_CTX, head), device_id_type=MESH)
    for hd in (zl * 4 + pa, zl * 4 + pb, (1 - zl) * 4 + y):
        pl.semaphore_signal(barrier, inc=1, device_id=(me, hd), device_id_type=MESH)
    pl.semaphore_wait(barrier, N_CTX - 1 + 3)

    lane = lax.broadcasted_iota(jnp.int32, (1, 128), 1)
    own_flags = jnp.where(lane == 0, flags_ref[0], jnp.where(lane == 1, flags_ref[1], 0))
    flag_src[...] = own_flags
    flag_all[me] = own_flags
    for i in range(1, N_CTX):
        sends.append(send(flag_src, flag_all.at[me], flag_send.at[i], flag_recv.at[me], ctx=(me + i) % N_CTX))
    for i in range(1, N_CTX):
        src = (me + i) % N_CTX
        await_recv(flag_all.at[src], flag_recv.at[src])
    to_scalars = pltpu.make_async_copy(flag_all, flag_sm, local_sem)
    to_scalars.start()
    to_scalars.wait()

    first_rank = jnp.int32(0)
    for i in range(N_CTX):
        first_rank += jnp.where(i < me, flag_sm[i, 0, 0] + flag_sm[i, 0, 1], 0)

    def shift_of(rank):
        return order_ref[rank] % N_CTX

    slot_span = (1 - flag_sm[me, 0, 0], jnp.int32(1))
    slot_shift = (shift_of(jnp.minimum(first_rank, KEPT - 1)), shift_of(jnp.minimum(first_rank + 1, KEPT - 1)))

    load_base.wait()
    load_hidden.wait()

    load_o.wait()
    half = pl.ds(core * 256, 256)
    other_half = pl.ds((1 - core) * 256, 256)
    cols_a, cols_b = pl.ds(0, 2048), pl.ds(2048, 2048)
    sends.append(send(wo.at[half, cols_a], wo_a.at[half, :], w_send.at[0], w_recv.at[0], hd=zl * 4 + pa))
    sends.append(send(wo.at[half, cols_b], wo_b.at[half, :], w_send.at[1], w_recv.at[1], hd=zl * 4 + pb))

    load_q.wait()
    load_k.wait()
    load_v.wait()

    def project_chunk(chunk, _):
        dx = (chunk + 1) % 4
        targets = [ctx_at(dz, dx, dc) for dz in (1, 0) for dc in (1, 0)]
        for slot in range(2):
            def norm_piece(i, _):
                target = ctx_at(1 - i // 2, dx, 1 - i % 2)
                piece = slot_span[slot] * 16 + (target + N_CTX - slot_shift[slot]) % N_CTX
                total = jnp.zeros((PIECE, 128), F32)
                for c in range(0, 4096, 512):
                    part = hidden[piece, :, c:c + 512].astype(F32)
                    part = part * part
                    total += (part[:, :128] + part[:, 128:256]) + (part[:, 256:384] + part[:, 384:])
                scale = lax.rsqrt(jnp.sum(total, axis=1, keepdims=True) * (1.0 / 4096) + 1e-05)
                dst = pl.ds(pl.multiple_of(i * 64 + slot * PIECE, PIECE), PIECE)
                for c in range(0, 4096, 512):
                    part = hidden[piece, :, c:c + 512].astype(F32)
                    normed[dst, c:c + 512] = (part * scale * gain_ref[:, c:c + 512]).astype(BF16)
                return 0
            lax.fori_loop(0, 4, norm_piece, 0)
        projected = jnp.dot(normed[...], wqkv[...], preferred_element_type=F32)
        for i, target in enumerate(targets):
            for slot in range(2):
                piece = slot_span[slot] * 16 + (target + N_CTX - slot_shift[slot]) % N_CTX
                cos_base, sin_base = base[piece, 0], base[piece, 1]
                cosine = cos_base * inner_ref[0] - sin_base * inner_ref[1]
                sine = sin_base * inner_ref[2] + cos_base * inner_ref[3]
                lo = i * 64 + slot * PIECE
                for part in range(6):
                    block = projected[lo:lo + PIECE, part * 128:(part + 1) * 128]
                    if part < 5:
                        block = block * cosine + pltpu.roll(block, 64, 1) * sine
                    stage[target, slot, part] = block.astype(BF16)
            if i < 3:
                send(stage.at[target], recv.at[me], a2a_send.at[target], a2a_recv.at[me], ctx=target)
            else:
                @pl.when(chunk < 3)
                def _():
                    send(stage.at[target], recv.at[me], a2a_send.at[target], a2a_recv.at[me], ctx=target)
        return 0

    lax.fori_loop(0, 4, project_chunk, 0)
    own = pltpu.make_async_copy(stage.at[me], recv.at[me], local_sem)
    own.start()

    arrival = [jnp.int32(0)] * KEPT
    rank = jnp.int32(0)
    for i in range(N_CTX):
        f0, f1 = flag_sm[i, 0, 0], flag_sm[i, 0, 1]
        for flag, place in ((f0, 2 * i), (f1, 2 * i + f0)):
            for r in range(KEPT):
                arrival[r] = jnp.where((flag == 1) & (rank == r), place, arrival[r])
            rank = rank + flag
    own.wait()
    for i in range(1, N_CTX):
        src = (me + i) % N_CTX
        await_recv(recv.at[src], a2a_recv.at[src])

    for r in range(KEPT):
        src, slot = arrival[r] // 2, arrival[r] % 2
        for part in range(4):
            queries[r * 128 + part * 32:r * 128 + part * 32 + 32, :] = recv[src, slot, part]
        rows = slice((r % 4) * 32, (r % 4) * 32 + 32)
        kv[r // 4, me, 0, rows, :] = recv[src, slot, 4]
        kv[r // 4, me, 1, rows, :] = recv[src, slot, 5]

    sibling = ctx_at(0, 0, 1)
    zmate = ctx_at(1, 0, 0)
    xplus, xminus = ctx_at(0, 1, 0), ctx_at(0, 3, 0)

    def pass_on(q, src, way, target):
        sends.append(send(kv.at[q, src], kv.at[q, src], kv_send.at[q, src, way], kv_recv.at[q, src], ctx=target))

    def arrived(q, src):
        await_recv(kv.at[q, src], kv_recv.at[q, src])

    for q in range(4):
        pass_on(q, me, 0, zmate)
    for q in range(4):
        pass_on(q, me, 1, xplus)
        pass_on(q, me, 2, xminus)
        pass_on(q, me, 3, sibling)
        arrived(q, zmate)
        pass_on(q, zmate, 1, xplus)
        pass_on(q, zmate, 2, xminus)
        pass_on(q, zmate, 3, sibling)
    for q in range(4):
        for dz in range(2):
            arrived(q, ctx_at(dz, 3, 0))
            if dz == 0:
                pass_on(q, ctx_at(dz, 3, 0), 1, xplus)
            pass_on(q, ctx_at(dz, 3, 0), 3, sibling)
            arrived(q, ctx_at(dz, 1, 0))
            if dz == 1:
                pass_on(q, ctx_at(dz, 1, 0), 2, xminus)
            pass_on(q, ctx_at(dz, 1, 0), 3, sibling)
    for q in range(4):
        for dz in range(2):
            arrived(q, ctx_at(dz, 2, 0))
            pass_on(q, ctx_at(dz, 2, 0), 3, sibling)
    await_recv(wo_a.at[half, :], w_recv.at[0])
    await_recv(wo_b.at[half, :], w_recv.at[1])
    sends.append(send(wo_a.at[half, :], wo_a.at[half, :], wc_send.at[0], wc_recv.at[0], ctx=sibling))
    sends.append(send(wo_b.at[half, :], wo_b.at[half, :], wc_send.at[1], wc_recv.at[1], ctx=sibling))
    for q in range(4):
        for dz in range(2):
            for dx in range(4):
                arrived(q, ctx_at(dz, dx, 1))

    factor = LOG2E / math.sqrt(HEAD_DIM)
    ones = jnp.ones((2048, 128), BF16)
    rows_block = 128
    key_lane = lax.broadcasted_iota(jnp.int32, (1, 2048), 1)

    def attend(g, q, masked):
        keys = kv[q, :, 0].reshape(2048, 128)
        values = jnp.concatenate([kv[q, :, 1].reshape(2048, 128), ones], axis=1)
        if masked:
            key_pos = jnp.zeros((1, 2048), jnp.int32)
            for b in range(4):
                place = (key_lane // 128 + N_CTX - shift_of(4 * q + b)) % N_CTX
                here = (key_lane % 128) // 32 == b
                key_pos = jnp.where(here, (4 * q + b) * SPAN + place * PIECE + key_lane % PIECE, key_pos)

        def block(a, _):
            rows = pl.ds(pl.multiple_of(g * 512 + a * rows_block, rows_block), rows_block)
            scores = lax.dot_general(queries[rows, :], keys, (((1,), (1,)), ((), ())), preferred_element_type=F32)
            if masked:
                r = 4 * g + a
                row = lax.broadcasted_iota(jnp.int32, (rows_block, 1), 0) % PIECE
                query_pos = r * SPAN + ((me + N_CTX - shift_of(r)) % N_CTX) * PIECE + row
                scores = jnp.where(key_pos <= query_pos, scores, -1e30)
            top = jnp.max(scores, axis=1, keepdims=True)
            if q == 0:
                new_peak = jnp.broadcast_to(top, (rows_block, 128))
            else:
                old = peak[rows, :]
                new_peak = jnp.maximum(old, top)
            expo = jnp.exp2((scores - new_peak[:, :1]) * factor).astype(BF16)
            mixed = jnp.dot(expo, values, preferred_element_type=F32)
            if q == 0:
                acc[rows, :] = mixed
            else:
                fade = jnp.exp2((old - new_peak) * factor)
                acc[rows, :] = acc[rows, :] * jnp.concatenate([fade, fade], axis=1) + mixed
            peak[rows, :] = new_peak
            return 0

        lax.fori_loop(0, 512 // rows_block, block, 0)

    for q in range(4):
        attend(q, q, True)
        if q < 3:
            def later(g, _, q=q):
                attend(g, q, False)
                return 0
            lax.fori_loop(q + 1, 4, later, 0)

    for r in range(KEPT):
        hd = r // 2
        for part in range(4):
            rows = slice(r * 128 + part * 32, r * 128 + part * 32 + 32)
            value = (acc[rows, :128] / acc[rows, 128:]).astype(BF16)
            att[hd % 4, hd // 4, (r % 2) * 32:(r % 2) * 32 + 32, part * 128:(part + 1) * 128] = value

    far = (y + 2) % 4
    at_pa, at_pb, at_z = zl * 4 + pa, zl * 4 + pb, (1 - zl) * 4 + y
    sends.append(send(att.at[far], att_a.at[1], att_send.at[0], att_recv.at[0], hd=at_pa))
    sends.append(send(att.at[far], att_b.at[1], att_send.at[1], att_recv.at[1], hd=at_pb))
    sends.append(send(att.at[pa], att_a.at[0], att_send.at[2], att_recv.at[2], hd=at_pa))
    sends.append(send(att.at[pb], att_b.at[0], att_send.at[3], att_recv.at[3], hd=at_pb))
    await_recv(wo_a.at[other_half, :], wc_recv.at[0])
    await_recv(wo_b.at[other_half, :], wc_recv.at[1])

    def term(rows_ref, weights):
        flat = rows_ref.reshape(128, 512)
        return jnp.dot(flat, weights, preferred_element_type=F32).astype(BF16).astype(F32)

    width = 512
    steps = 2048 // width
    await_recv(att_a.at[1], att_recv.at[0])
    await_recv(att_b.at[1], att_recv.at[1])

    def far_step(c, _):
        cols = pl.ds(pl.multiple_of(c * width, width), width)
        cols_far = pl.ds(pl.multiple_of(2048 + c * width, width), width)
        total = term(att[pb], wo[:, cols]) + term(att_a[1], wo_a[:, cols])
        part_a[c] = total.astype(BF16)
        send(part_a.at[c], got_a.at[c], part_send.at[0, c], part_recv.at[0, c], hd=at_pb)
        total = term(att[pa], wo[:, cols_far]) + term(att_b[1], wo_b[:, cols])
        part_b[c] = total.astype(BF16)
        send(part_b.at[c], got_b.at[c], part_send.at[1, c], part_recv.at[1, c], hd=at_pa)
        return 0

    lax.fori_loop(0, steps, far_step, 0)
    await_recv(att_a.at[0], att_recv.at[2])
    await_recv(att_b.at[0], att_recv.at[3])

    def near_step(c, _):
        cols = pl.ds(pl.multiple_of(c * width, width), width)
        cols_far = pl.ds(pl.multiple_of(2048 + c * width, width), width)
        mine[c] = term(att[y], wo[:, cols]) + term(att_a[0], wo_a[:, cols])
        mine[steps + c] = term(att[y], wo[:, cols_far]) + term(att_b[0], wo_b[:, cols])
        return 0

    lax.fori_loop(0, steps, near_step, 0)

    z_rows = pl.ds(pl.multiple_of((1 - zl) * 64, 64), 64)
    own_rows = pl.ds(pl.multiple_of(zl * 64, 64), 64)

    def sum_step(c, _):
        for side, got in ((0, got_a), (1, got_b)):
            slot = side * steps + c
            await_recv(got.at[c], part_recv.at[side, c])
            mine[slot] = mine[slot] + got[c].astype(F32)
            zsend[slot] = mine[slot, z_rows, :].astype(BF16)
            send(zsend.at[slot], zgot.at[slot], z_send.at[slot], z_recv.at[slot], hd=at_z)
        return 0

    lax.fori_loop(0, steps, sum_step, 0)

    def final_step(slot, _):
        await_recv(zgot.at[slot], z_recv.at[slot])
        cols = pl.ds(pl.multiple_of(slot * width, width), width)
        out_ref[:, cols] = (mine[slot, own_rows, :] + zgot[slot].astype(F32)).astype(BF16)
        return 0

    lax.fori_loop(0, 2 * steps, final_step, 0)

    for copy in sends:
        copy.wait_send()

    def await_send(src, ssem):
        pltpu.make_async_remote_copy(
            src_ref=src, dst_ref=src, send_sem=ssem, recv_sem=ssem,
            device_id=(me, head), device_id_type=MESH,
        ).wait_send()

    for i in range(1, N_CTX):
        target = (me + i) % N_CTX
        await_send(stage.at[target], a2a_send.at[target])

    def drain(c, _):
        await_send(part_a.at[c], part_send.at[0, c])
        await_send(part_b.at[c], part_send.at[1, c])
        await_send(zsend.at[c], z_send.at[c])
        await_send(zsend.at[steps + c], z_send.at[steps + c])
        return 0

    lax.fori_loop(0, steps, drain, 0)


def body(hidden_states, norm_gain, query_weight, key_weight, value_weight, output_weight, keep_flags, span_order):
    base, inner = rope_tables()
    vmem = pl.BlockSpec(memory_space=pltpu.VMEM)
    smem = pl.BlockSpec(memory_space=pltpu.SMEM)
    anywhere = pl.BlockSpec(memory_space=pl.ANY)
    dma = pltpu.SemaphoreType.DMA
    return pl.pallas_call(
        kernel,
        out_shape=jax.ShapeDtypeStruct((64, 4096), BF16),
        in_specs=[anywhere, vmem, anywhere, anywhere, anywhere, anywhere, smem, smem, anywhere, vmem],
        out_specs=vmem,
        scratch_shapes=[
            pltpu.VMEM((32, 32, 4096), BF16),
            pltpu.VMEM((4096, 768), BF16),
            pltpu.VMEM((512, 4096), BF16),
            pltpu.VMEM((512, 2048), BF16),
            pltpu.VMEM((512, 2048), BF16),
            pltpu.VMEM((32, 2, 1, 128), F32),
            pltpu.VMEM((256, 4096), BF16),
            pltpu.VMEM((1, 128), jnp.int32),
            pltpu.VMEM((16, 1, 128), jnp.int32),
            pltpu.SMEM((16, 1, 128), jnp.int32),
            pltpu.VMEM((16, 2, 6, 32, 128), BF16),
            pltpu.VMEM((16, 2, 6, 32, 128), BF16),
            pltpu.VMEM((2048, 128), BF16),
            pltpu.VMEM((4, 16, 2, 128, 128), BF16),
            pltpu.VMEM((2048, 256), F32),
            pltpu.VMEM((2048, 128), F32),
            pltpu.VMEM((4, 2, 64, 512), BF16),
            pltpu.VMEM((2, 2, 64, 512), BF16),
            pltpu.VMEM((2, 2, 64, 512), BF16),
            pltpu.VMEM((4, 128, 512), BF16),
            pltpu.VMEM((4, 128, 512), BF16),
            pltpu.VMEM((4, 128, 512), BF16),
            pltpu.VMEM((4, 128, 512), BF16),
            pltpu.VMEM((8, 128, 512), F32),
            pltpu.VMEM((8, 64, 512), BF16),
            pltpu.VMEM((8, 64, 512), BF16),
            dma((8,)),
            dma((16,)), dma((16,)),
            dma((16,)), dma((16,)),
            dma((4, 16, 4)), dma((4, 16)),
            dma((2,)), dma((2,)), dma((2,)), dma((2,)),
            dma((4,)), dma((4,)),
            dma((2, 4)), dma((2, 4)),
            dma((8,)), dma((8,)),
            dma,
        ],
        compiler_params=pltpu.CompilerParams(
            collective_id=1, has_side_effects=True, vmem_limit_bytes=60 * 2**20
        ),
        name="prefill",
    )(
        hidden_states.reshape(32, 32, 4096), norm_gain.reshape(1, 4096), query_weight, key_weight, value_weight, output_weight,
        keep_flags, span_order, jnp.asarray(base), jnp.asarray(inner),
    )


def solution(mesh):
    return jax.shard_map(
        body,
        mesh=mesh,
        in_specs=(
            P("ctx", None),
            P(),
            P(None, "head"),
            P(None, "head"),
            P(None, "head"),
            P("head", None),
            P("ctx"),
            P(),
        ),
        out_specs=P(("ctx", "head"), None),
        check_vma=False,
    )
```

time: 421 us -> 133 us (0.32)
  waiting for transfers between devices: 169 us -> 0 us
  matrix products: 156 us -> 0 us
  Pallas kernels: 0 us -> 129 us
  other arithmetic: 47.6 us -> 0 us
  between operations: 14.1 us -> 0.01 us
  blocking collectives: 13.8 us -> 0 us
  local copies, waits for them, and re-layouts: 13 us -> 1.87 us
    dot_general x36 -> x0, matrix products: 156 us -> none  [the longest x16 69 us: advance(): jnp.einsum('kgqn,nkd->kgqd', expo.astype(jnp.bfloat16), value_block, pref...]
    pallas_call x0 -> x1, Pallas kernels: none -> 129 us  [body(): pl.pallas_call(kernel, out_shape=jax.ShapeDtypeStruct((64, 4096), BF16),...]
    all_gather x2 -> x0, waiting for transfers between devices: 94 us -> none  [the longest x1 49.6 us: body(): value_piece = lax.all_gather(value_states, 'ctx', axis=0, tiled=True)]
    reduce_scatter x1 -> x0, waiting for transfers between devices: 51.8 us -> none  [body(): lax.psum_scatter(jnp.dot(attended, output_weight, preferred_element_type=...]
    reduce_sum x26 -> x0, other arithmetic: 24.3 us -> none  [the longest x16 16.8 us: advance(): denominator = denominator * rescale + jnp.sum(expo, axis=3)]
    all_to_all x1 -> x0, waiting for transfers between devices: 22.4 us -> none  [body(): lax.all_to_all(jnp.where(slot_valid[None, :, None, None], gathered, jnp.z...]
    unnamed x1 -> x0, blocking collectives: 13.8 us -> none
    convert_element_type x4 -> x0, other arithmetic: 10.5 us -> none  [the longest x1 10.3 us: rms_normed(): (widened * lax.rsqrt(mean_square + 1e-05) * norm_gain).astype(jnp.bfloat16)]
  transfers between devices with their start and end apart: 4 -> 0, of which waited for: 4 -> 0; matrix products, arithmetic and copies ran while one was open for 0% -> 0% of each run, Pallas kernels for 0% -> 0%
where the time goes in v1:
time: 133 us; the launch traced here: 131 us
  Pallas kernels  129 us (97%)
  local copies, waits for them, and re-layouts  1.87 us (1%)
    pallas_call x1, Pallas kernels, body(): pl.pallas_call(kernel, out_shape=jax.ShapeDtypeStruct((64, 4096), BF16),...  129 us

profile of v1, /device:TPU:32, one launch (start us, length us, event | category | flops | bytes accessed | tf_op | source)
XLA Modules:
  0.0 130.6 jit_solution(17687635246530500408)
XLA Ops:
  0.0 128.8 %prefill.1 = bf16[64,4096]{1,0:T(8,128)(2,1)} custom-call(bf16[32,32,4096]{2,1,0:T(8,128)(2,1)} %bitcast.2, f32[1,4096]{1,0:T(1,128)} %bitcast.3, bf16[4096,512]{1,0:T(8,128)(2,1)} %wq_hbm.1, bf16[4096,128]{1,0:T(8,128)(2,1)} %wk_hbm.1, bf16[4096,128]{1,0:T(8,128)(2,1)} %wv_hbm.1, bf16[512,4096]{1,0:T(8,128)(2,1)} %wo_hbm.1, s32[2]{0:T(128)} %flags_ref.1, ...), custom_call_target="tpu_custom_call" | custom-call | tf_op jit(solution)/shard_map/prefill/pallas_call | solution.py:385
  128.8 1.9 %copy.12 = bf16[64,4096]{1,0:T(8,128)(2,1)} copy(bf16[64,4096]{1,0:T(8,128)(2,1)} %prefill.1) | data formatting | bytes 1048576

commit v2 on v1

--- a/solution.py
+++ b/solution.py
@@ -195,160 +195,226 @@
     xplus, xminus = ctx_at(0, 1, 0), ctx_at(0, 3, 0)
 
     def pass_on(q, src, way, target):
-        sends.append(send(kv.at[q, src], kv.at[q, src], kv_send.at[q, src, way], kv_recv.at[q, src], ctx=target))
+        send(kv.at[q, src], kv.at[q, src], kv_send.at[q, src, way], kv_recv.at[q, src], ctx=target)
 
     def arrived(q, src):
         await_recv(kv.at[q, src], kv_recv.at[q, src])
 
-    for q in range(4):
-        pass_on(q, me, 0, zmate)
-    for q in range(4):
+    def gather_own(q):
         pass_on(q, me, 1, xplus)
         pass_on(q, me, 2, xminus)
         pass_on(q, me, 3, sibling)
+
+    def gather_mate(q):
         arrived(q, zmate)
         pass_on(q, zmate, 1, xplus)
         pass_on(q, zmate, 2, xminus)
         pass_on(q, zmate, 3, sibling)
-    for q in range(4):
+
+    def gather_near(q):
         for dz in range(2):
-            arrived(q, ctx_at(dz, 3, 0))
+            left, right = ctx_at(dz, 3, 0), ctx_at(dz, 1, 0)
+            arrived(q, left)
             if dz == 0:
-                pass_on(q, ctx_at(dz, 3, 0), 1, xplus)
-            pass_on(q, ctx_at(dz, 3, 0), 3, sibling)
-            arrived(q, ctx_at(dz, 1, 0))
+                pass_on(q, left, 1, xplus)
+            pass_on(q, left, 3, sibling)
+            arrived(q, right)
             if dz == 1:
-                pass_on(q, ctx_at(dz, 1, 0), 2, xminus)
-            pass_on(q, ctx_at(dz, 1, 0), 3, sibling)
-    for q in range(4):
+                pass_on(q, right, 2, xminus)
+            pass_on(q, right, 3, sibling)
+
+    def gather_far(q):
         for dz in range(2):
-            arrived(q, ctx_at(dz, 2, 0))
-            pass_on(q, ctx_at(dz, 2, 0), 3, sibling)
-    await_recv(wo_a.at[half, :], w_recv.at[0])
-    await_recv(wo_b.at[half, :], w_recv.at[1])
-    sends.append(send(wo_a.at[half, :], wo_a.at[half, :], wc_send.at[0], wc_recv.at[0], ctx=sibling))
-    sends.append(send(wo_b.at[half, :], wo_b.at[half, :], wc_send.at[1], wc_recv.at[1], ctx=sibling))
-    for q in range(4):
+            across = ctx_at(dz, 2, 0)
+            arrived(q, across)
+            pass_on(q, across, 3, sibling)
+
+    def gather_end(q):
         for dz in range(2):
             for dx in range(4):
                 arrived(q, ctx_at(dz, dx, 1))
 
     factor = LOG2E / math.sqrt(HEAD_DIM)
-    ones = jnp.ones((2048, 128), BF16)
-    rows_block = 128
-    key_lane = lax.broadcasted_iota(jnp.int32, (1, 2048), 1)
+    block_rows = 128
+    blocks = 512 // block_rows
 
     def attend(g, q, masked):
         keys = kv[q, :, 0].reshape(2048, 128)
-        values = jnp.concatenate([kv[q, :, 1].reshape(2048, 128), ones], axis=1)
+        values = jnp.concatenate([kv[q, :, 1].reshape(2048, 128), jnp.ones((2048, 128), BF16)], axis=1)
         if masked:
+            key_lane = lax.broadcasted_iota(jnp.int32, (1, 2048), 1)
             key_pos = jnp.zeros((1, 2048), jnp.int32)
             for b in range(4):
                 place = (key_lane // 128 + N_CTX - shift_of(4 * q + b)) % N_CTX
                 here = (key_lane % 128) // 32 == b
-                key_pos = jnp.where(here, (4 * q + b) * SPAN + place * PIECE + key_lane % PIECE, key_pos)
-
-        def block(a, _):
-            rows = pl.ds(pl.multiple_of(g * 512 + a * rows_block, rows_block), rows_block)
-            scores = lax.dot_general(queries[rows, :], keys, (((1,), (1,)), ((), ())), preferred_element_type=F32)
+                key_pos = jnp.where(here, b * SPAN + place * PIECE + key_lane % PIECE, key_pos)
+
+        def rows_of(a):
+            return pl.ds(pl.multiple_of(g * 512 + a * block_rows, block_rows), block_rows)
+
+        def score(a):
+            return lax.dot_general(
+                queries[rows_of(a), :], keys, (((1,), (1,)), ((), ())), preferred_element_type=F32
+            )
+
+        scores = score(0)
+        for a in range(blocks):
+            rows = rows_of(a)
+            coming = score(a + 1) if a + 1 < blocks else None
             if masked:
-                r = 4 * g + a
-                row = lax.broadcasted_iota(jnp.int32, (rows_block, 1), 0) % PIECE
-                query_pos = r * SPAN + ((me + N_CTX - shift_of(r)) % N_CTX) * PIECE + row
+                row = lax.broadcasted_iota(jnp.int32, (block_rows, 1), 0) % PIECE
+                query_pos = a * SPAN + ((me + N_CTX - shift_of(4 * q + a)) % N_CTX) * PIECE + row
                 scores = jnp.where(key_pos <= query_pos, scores, -1e30)
-            top = jnp.max(scores, axis=1, keepdims=True)
-            if q == 0:
-                new_peak = jnp.broadcast_to(top, (rows_block, 128))
-            else:
-                old = peak[rows, :]
-                new_peak = jnp.maximum(old, top)
-            expo = jnp.exp2((scores - new_peak[:, :1]) * factor).astype(BF16)
+            old = peak[rows, :]
+            new = jnp.maximum(old, jnp.max(scores, axis=1, keepdims=True))
+            peak[rows, :] = new
+            expo = jnp.exp2((scores - new[:, :1]) * factor).astype(BF16)
+            fade = jnp.exp2((old - new) * factor)
             mixed = jnp.dot(expo, values, preferred_element_type=F32)
-            if q == 0:
-                acc[rows, :] = mixed
-            else:
-                fade = jnp.exp2((old - new_peak) * factor)
-                acc[rows, :] = acc[rows, :] * jnp.concatenate([fade, fade], axis=1) + mixed
-            peak[rows, :] = new_peak
-            return 0
-
-        lax.fori_loop(0, 512 // rows_block, block, 0)
-
-    for q in range(4):
-        attend(q, q, True)
-        if q < 3:
-            def later(g, _, q=q):
-                attend(g, q, False)
-                return 0
-            lax.fori_loop(q + 1, 4, later, 0)
-
-    for r in range(KEPT):
-        hd = r // 2
-        for part in range(4):
-            rows = slice(r * 128 + part * 32, r * 128 + part * 32 + 32)
-            value = (acc[rows, :128] / acc[rows, 128:]).astype(BF16)
-            att[hd % 4, hd // 4, (r % 2) * 32:(r % 2) * 32 + 32, part * 128:(part + 1) * 128] = value
+            acc[rows, :] = acc[rows, :] * jnp.concatenate([fade, fade], axis=1) + mixed
+            scores = coming
+
+    def finish(g):
+        for r in range(4 * g, 4 * g + 4):
+            hd = r // 2
+            for part in range(4):
+                rows = slice(r * 128 + part * 32, r * 128 + part * 32 + 32)
+                value = (acc[rows, :128] / acc[rows, 128:]).astype(BF16)
+                att[hd % 4, hd // 4, (r % 2) * 32:(r % 2) * 32 + 32, part * 128:(part + 1) * 128] = value
 
     far = (y + 2) % 4
     at_pa, at_pb, at_z = zl * 4 + pa, zl * 4 + pb, (1 - zl) * 4 + y
-    sends.append(send(att.at[far], att_a.at[1], att_send.at[0], att_recv.at[0], hd=at_pa))
-    sends.append(send(att.at[far], att_b.at[1], att_send.at[1], att_recv.at[1], hd=at_pb))
-    sends.append(send(att.at[pa], att_a.at[0], att_send.at[2], att_recv.at[2], hd=at_pa))
-    sends.append(send(att.at[pb], att_b.at[0], att_send.at[3], att_recv.at[3], hd=at_pb))
-    await_recv(wo_a.at[other_half, :], wc_recv.at[0])
-    await_recv(wo_b.at[other_half, :], wc_recv.at[1])
-
-    def term(rows_ref, weights):
-        flat = rows_ref.reshape(128, 512)
-        return jnp.dot(flat, weights, preferred_element_type=F32).astype(BF16).astype(F32)
+    att_moves = ((far, att_a, 1, at_pa), (far, att_b, 1, at_pb), (pa, att_a, 0, at_pa), (pb, att_b, 0, at_pb))
+
+    def exchange(z):
+        for i, (block, dst, slot, hd) in enumerate(att_moves):
+            send(att.at[block, z], dst.at[slot, z], att_send.at[z, i], att_recv.at[z, i], hd=hd)
+
+    def term(rows, weights):
+        return jnp.dot(rows, weights, preferred_element_type=F32).astype(BF16).astype(F32)
 
     width = 512
     steps = 2048 // width
-    await_recv(att_a.at[1], att_recv.at[0])
-    await_recv(att_b.at[1], att_recv.at[1])
-
-    def far_step(c, _):
-        cols = pl.ds(pl.multiple_of(c * width, width), width)
-        cols_far = pl.ds(pl.multiple_of(2048 + c * width, width), width)
-        total = term(att[pb], wo[:, cols]) + term(att_a[1], wo_a[:, cols])
-        part_a[c] = total.astype(BF16)
-        send(part_a.at[c], got_a.at[c], part_send.at[0, c], part_recv.at[0, c], hd=at_pb)
-        total = term(att[pa], wo[:, cols_far]) + term(att_b[1], wo_b[:, cols])
-        part_b[c] = total.astype(BF16)
-        send(part_b.at[c], got_b.at[c], part_send.at[1, c], part_recv.at[1, c], hd=at_pa)
+
+    def two_cols(c):
+        return (
+            pl.ds(pl.multiple_of(c * width, width), width),
+            pl.ds(pl.multiple_of(2048 + c * width, width), width),
+        )
+
+    def project_far(z):
+        await_recv(att_a.at[1, z], att_recv.at[z, 0])
+        await_recv(att_b.at[1, z], att_recv.at[z, 1])
+
+        def step(c, _):
+            cols, cols_b = two_cols(c)
+            total = term(att[pb, z], wo[:, cols]) + term(att_a[1, z], wo_a[:, cols])
+            part_a[z, c] = total.astype(BF16)
+            send(part_a.at[z, c], got_a.at[z, c], part_send.at[z, 0, c], part_recv.at[z, 0, c], hd=at_pb)
+            total = term(att[pa, z], wo[:, cols_b]) + term(att_b[1, z], wo_b[:, cols])
+            part_b[z, c] = total.astype(BF16)
+            send(part_b.at[z, c], got_b.at[z, c], part_send.at[z, 1, c], part_recv.at[z, 1, c], hd=at_pa)
+            return 0
+
+        lax.fori_loop(0, steps, step, 0)
+
+    def project_near(z):
+        await_recv(att_a.at[0, z], att_recv.at[z, 2])
+        await_recv(att_b.at[0, z], att_recv.at[z, 3])
+
+        def step(c, _):
+            cols, cols_b = two_cols(c)
+            mine[z, c] = term(att[y, z], wo[:, cols]) + term(att_a[0, z], wo_a[:, cols])
+            mine[z, steps + c] = term(att[y, z], wo[:, cols_b]) + term(att_b[0, z], wo_b[:, cols])
+            return 0
+
+        lax.fori_loop(0, steps, step, 0)
+
+    def sum_up(z):
+        def step(c, _):
+            for side, got in ((0, got_a), (1, got_b)):
+                slot = side * steps + c
+                await_recv(got.at[z, c], part_recv.at[z, side, c])
+                total = mine[z, slot] + got[z, c].astype(F32)
+
+                @pl.when(zl == z)
+                def _():
+                    mine[z, slot] = total
+
+                @pl.when(zl != z)
+                def _():
+                    zsend[slot] = total.astype(BF16)
+                    send(zsend.at[slot], zgot.at[slot], z_send.at[slot], z_recv.at[slot], hd=at_z)
+            return 0
+
+        lax.fori_loop(0, steps, step, 0)
+
+    def weights_across():
+        await_recv(wo_a.at[half, :], w_recv.at[0])
+        await_recv(wo_b.at[half, :], w_recv.at[1])
+        send(wo_a.at[half, :], wo_a.at[half, :], wc_send.at[0], wc_recv.at[0], ctx=sibling)
+        send(wo_b.at[half, :], wo_b.at[half, :], wc_send.at[1], wc_recv.at[1], ctx=sibling)
+
+    def weights_end():
+        await_recv(wo_a.at[other_half, :], wc_recv.at[0])
+        await_recv(wo_b.at[other_half, :], wc_recv.at[1])
+
+    for q in range(4):
+        pass_on(q, me, 0, zmate)
+    acc[...] = jnp.zeros_like(acc)
+    peak[...] = jnp.full(peak.shape, -1e30, F32)
+    gather_own(0)
+    gather_mate(0)
+    gather_own(1)
+    gather_mate(1)
+    gather_near(0)
+    gather_own(2)
+    gather_mate(2)
+    gather_far(0)
+    gather_end(0)
+
+    plan = ((0, 0), (1, 0), (2, 0), (3, 0), (1, 1), (2, 1), (3, 1), (2, 2), (3, 2), (3, 3))
+    after = {
+        0: lambda: (gather_near(1), weights_across()),
+        1: lambda: (gather_own(3), gather_mate(3), gather_far(1)),
+        2: lambda: gather_near(2),
+        3: lambda: (gather_end(1), weights_end()),
+        4: lambda: (finish(0), finish(1), exchange(0), gather_far(2), gather_near(3)),
+        6: lambda: (gather_end(2), project_far(0)),
+        7: lambda: (finish(2), gather_far(3), project_near(0)),
+        8: lambda: (gather_end(3), sum_up(0)),
+    }
+
+    def attention_step(i, _):
+        g, q = jnp.int32(0), jnp.int32(0)
+        for k, (gk, qk) in enumerate(plan):
+            g, q = jnp.where(i == k, gk, g), jnp.where(i == k, qk, q)
+
+        @pl.when(g == q)
+        def _():
+            attend(g, q, True)
+
+        @pl.when(g != q)
+        def _():
+            attend(g, q, False)
+
+        for k, work in after.items():
+            pl.when(i == k)(lambda work=work: (work(), None)[1])
         return 0
 
-    lax.fori_loop(0, steps, far_step, 0)
-    await_recv(att_a.at[0], att_recv.at[2])
-    await_recv(att_b.at[0], att_recv.at[3])
-
-    def near_step(c, _):
-        cols = pl.ds(pl.multiple_of(c * width, width), width)
-        cols_far = pl.ds(pl.multiple_of(2048 + c * width, width), width)
-        mine[c] = term(att[y], wo[:, cols]) + term(att_a[0], wo_a[:, cols])
-        mine[steps + c] = term(att[y], wo[:, cols_far]) + term(att_b[0], wo_b[:, cols])
-        return 0
-
-    lax.fori_loop(0, steps, near_step, 0)
-
-    z_rows = pl.ds(pl.multiple_of((1 - zl) * 64, 64), 64)
-    own_rows = pl.ds(pl.multiple_of(zl * 64, 64), 64)
-
-    def sum_step(c, _):
-        for side, got in ((0, got_a), (1, got_b)):
-            slot = side * steps + c
-            await_recv(got.at[c], part_recv.at[side, c])
-            mine[slot] = mine[slot] + got[c].astype(F32)
-            zsend[slot] = mine[slot, z_rows, :].astype(BF16)
-            send(zsend.at[slot], zgot.at[slot], z_send.at[slot], z_recv.at[slot], hd=at_z)
-        return 0
-
-    lax.fori_loop(0, steps, sum_step, 0)
+    lax.fori_loop(0, len(plan), attention_step, 0)
+    finish(3)
+    exchange(1)
+    project_far(1)
+    project_near(1)
+    sum_up(1)
+
+    own_rows = zl
 
     def final_step(slot, _):
         await_recv(zgot.at[slot], z_recv.at[slot])
         cols = pl.ds(pl.multiple_of(slot * width, width), width)
-        out_ref[:, cols] = (mine[slot, own_rows, :] + zgot[slot].astype(F32)).astype(BF16)
+        out_ref[:, cols] = (mine[own_rows, slot] + zgot[slot].astype(F32)).astype(BF16)
         return 0
 
     lax.fori_loop(0, 2 * steps, final_step, 0)
@@ -366,9 +432,28 @@
         target = (me + i) % N_CTX
         await_send(stage.at[target], a2a_send.at[target])
 
+    def drain_kv(q, _):
+        for way in range(4):
+            await_send(kv.at[q, me], kv_send.at[q, me, way])
+        for way in range(1, 4):
+            await_send(kv.at[q, zmate], kv_send.at[q, zmate, way])
+        for dz in range(2):
+            for dx in range(1, 4):
+                src = ctx_at(dz, dx, 0)
+                await_send(kv.at[q, src], kv_send.at[q, src, 3])
+        await_send(kv.at[q, ctx_at(0, 3, 0)], kv_send.at[q, ctx_at(0, 3, 0), 1])
+        await_send(kv.at[q, ctx_at(1, 1, 0)], kv_send.at[q, ctx_at(1, 1, 0), 2])
+        return 0
+
+    lax.fori_loop(0, 4, drain_kv, 0)
+    await_send(wo_a.at[half, :], wc_send.at[0])
+    await_send(wo_b.at[half, :], wc_send.at[1])
+
     def drain(c, _):
-        await_send(part_a.at[c], part_send.at[0, c])
-        await_send(part_b.at[c], part_send.at[1, c])
+        for z in range(2):
+            await_send(part_a.at[z, c], part_send.at[z, 0, c])
+            await_send(part_b.at[z, c], part_send.at[z, 1, c])
+            await_send(att.at[0, 0], att_send.at[z, c])
         await_send(zsend.at[c], z_send.at[c])
         await_send(zsend.at[steps + c], z_send.at[steps + c])
         return 0
@@ -407,11 +492,11 @@
             pltpu.VMEM((4, 2, 64, 512), BF16),
             pltpu.VMEM((2, 2, 64, 512), BF16),
             pltpu.VMEM((2, 2, 64, 512), BF16),
-            pltpu.VMEM((4, 128, 512), BF16),
-            pltpu.VMEM((4, 128, 512), BF16),
-            pltpu.VMEM((4, 128, 512), BF16),
-            pltpu.VMEM((4, 128, 512), BF16),
-            pltpu.VMEM((8, 128, 512), F32),
+            pltpu.VMEM((2, 4, 64, 512), BF16),
+            pltpu.VMEM((2, 4, 64, 512), BF16),
+            pltpu.VMEM((2, 4, 64, 512), BF16),
+            pltpu.VMEM((2, 4, 64, 512), BF16),
+            pltpu.VMEM((2, 8, 64, 512), F32),
             pltpu.VMEM((8, 64, 512), BF16),
             pltpu.VMEM((8, 64, 512), BF16),
             dma((8,)),
@@ -419,8 +504,8 @@
             dma((16,)), dma((16,)),
             dma((4, 16, 4)), dma((4, 16)),
             dma((2,)), dma((2,)), dma((2,)), dma((2,)),
-            dma((4,)), dma((4,)),
             dma((2, 4)), dma((2, 4)),
+            dma((2, 2, 4)), dma((2, 2, 4)),
             dma((8,)), dma((8,)),
             dma,
         ],

time: 133 us -> 109 us (0.82); the launches traced: 131 us -> 109 us
  Pallas kernels: 129 us -> 107 us
    pallas_call x1, Pallas kernels: 129 us -> 107 us  [body(): pl.pallas_call(kernel, out_shape=jax.ShapeDtypeStruct((64, 4096), BF16),...]
where the time goes in v2:
time: 109 us
  Pallas kernels  107 us (98%)
  local copies, waits for them, and re-layouts  1.87 us (2%)
    pallas_call x1, Pallas kernels, body(): pl.pallas_call(kernel, out_shape=jax.ShapeDtypeStruct((64, 4096), BF16),...  107 us

profile of v2, /device:TPU:32, one launch (start us, length us, event | category | flops | bytes accessed | tf_op | source)
XLA Modules:
  0.0 109.0 jit_solution(16206371598039493711)
XLA Ops:
  0.0 107.1 %prefill.1 = bf16[64,4096]{1,0:T(8,128)(2,1)} custom-call(bf16[32,32,4096]{2,1,0:T(8,128)(2,1)} %bitcast.2, f32[1,4096]{1,0:T(1,128)} %bitcast.3, bf16[4096,512]{1,0:T(8,128)(2,1)} %wq_hbm.1, bf16[4096,128]{1,0:T(8,128)(2,1)} %wk_hbm.1, bf16[4096,128]{1,0:T(8,128)(2,1)} %wv_hbm.1, bf16[512,4096]{1,0:T(8,128)(2,1)} %wo_hbm.1, s32[2]{0:T(128)} %flags_ref.1, ...), custom_call_target="tpu_custom_call" | custom-call | tf_op jit(solution)/shard_map/prefill/pallas_call | solution.py:470
  107.1 1.9 %copy.12 = bf16[64,4096]{1,0:T(8,128)(2,1)} copy(bf16[64,4096]{1,0:T(8,128)(2,1)} %prefill.1) | data formatting | bytes 1048576

commit v3 on v2

--- a/solution.py
+++ b/solution.py
@@ -34,9 +34,10 @@
 def kernel(
     hidden_hbm, gain_ref, wq_hbm, wk_hbm, wv_hbm, wo_hbm, flags_ref, order_ref, base_hbm, inner_ref,
     out_ref,
-    hidden, wqkv, wo, wo_a, wo_b, base, normed, flag_src, flag_all, flag_sm, stage, recv,
+    hidden, wq, wkv, wo, wo_a, wo_b, base, normed, flag_src, flag_all, flag_sm,
+    kv_raw, q_raw, kv_stage, q_stage, kv_got, q_got,
     queries, kv, acc, peak, att, att_a, att_b, part_a, part_b, got_a, got_b, mine, zsend, zgot,
-    load_sem, flag_send, flag_recv, a2a_send, a2a_recv, kv_send, kv_recv, w_send, w_recv, wc_send, wc_recv,
+    hidden_sem, load_sem, flag_send, flag_recv, kva_send, kva_recv, qa_send, qa_recv, kv_send, kv_recv, w_send, w_recv, wc_send, wc_recv,
     att_send, att_recv, part_send, part_recv, z_send, z_recv, local_sem,
 ):
     me = lax.axis_index("ctx")
@@ -66,6 +67,10 @@
 
     sends = []
 
+    def hidden_part(c):
+        part = pl.ds(c * 8, 8)
+        return pltpu.make_async_copy(hidden_hbm.at[part], hidden.at[part], hidden_sem.at[c])
+
     loads = []
 
     def load(src, dst):
@@ -74,11 +79,13 @@
         loads.append(copy)
         return copy
 
+    hidden_part(0).start()
+    load_k = load(wk_hbm, wkv.at[:, pl.ds(0, 128)])
+    load_v = load(wv_hbm, wkv.at[:, pl.ds(128, 128)])
     load_base = load(base_hbm.at[me], base)
-    load_hidden = load(hidden_hbm, hidden)
-    load_q = load(wq_hbm, wqkv.at[:, pl.ds(0, 512)])
-    load_k = load(wk_hbm, wqkv.at[:, pl.ds(512, 128)])
-    load_v = load(wv_hbm, wqkv.at[:, pl.ds(640, 128)])
+    for c in range(1, 4):
+        hidden_part(c).start()
+    load_q = load(wq_hbm, wq)
     load_o = load(wo_hbm, wo)
 
     barrier = pltpu.get_barrier_semaphore()
@@ -94,6 +101,53 @@
     flag_all[me] = own_flags
     for i in range(1, N_CTX):
         sends.append(send(flag_src, flag_all.at[me], flag_send.at[i], flag_recv.at[me], ctx=(me + i) % N_CTX))
+
+    load_base.wait()
+    load_k.wait()
+    load_v.wait()
+
+    def rope_of(piece):
+        cos_base, sin_base = base[piece, 0], base[piece, 1]
+        return (
+            cos_base * inner_ref[0] - sin_base * inner_ref[1],
+            sin_base * inner_ref[2] + cos_base * inner_ref[3],
+        )
+
+    def turned(block, rope):
+        return (block * rope[0] + pltpu.roll(block, 64, 1) * rope[1]).astype(BF16)
+
+    def norm_piece(piece, _):
+        total = jnp.zeros((PIECE, 128), F32)
+        for c in range(0, 4096, 512):
+            part = hidden[piece, :, c:c + 512].astype(F32)
+            part = part * part
+            total += (part[:, :128] + part[:, 128:256]) + (part[:, 256:384] + part[:, 384:])
+        scale = lax.rsqrt(jnp.sum(total, axis=1, keepdims=True) * (1.0 / 4096) + 1e-05)
+        for c in range(0, 4096, 512):
+            part = hidden[piece, :, c:c + 512].astype(F32)
+            normed[piece, :, c:c + 512] = (part * scale * gain_ref[:, c:c + 512]).astype(BF16)
+        return 0
+
+    def project_kv(c, _):
+        hidden_part(c).wait()
+        lax.fori_loop(c * 8, c * 8 + 8, norm_piece, 0)
+        rows = normed[pl.ds(c * 8, 8)].reshape(256, 4096)
+        projected = jnp.dot(rows, wkv[...], preferred_element_type=F32)
+        for i in range(8):
+            block = projected[i * PIECE:(i + 1) * PIECE]
+            kv_raw[c * 8 + i, 0] = turned(block[:, :128], rope_of(c * 8 + i))
+            kv_raw[c * 8 + i, 1] = block[:, 128:].astype(BF16)
+        return 0
+
+    lax.fori_loop(0, 4, project_kv, 0)
+
+    load_o.wait()
+    half = pl.ds(core * 256, 256)
+    other_half = pl.ds((1 - core) * 256, 256)
+    cols_a, cols_b = pl.ds(0, 2048), pl.ds(2048, 2048)
+    sends.append(send(wo.at[half, cols_a], wo_a.at[half, :], w_send.at[0], w_recv.at[0], hd=zl * 4 + pa))
+    sends.append(send(wo.at[half, cols_b], wo_b.at[half, :], w_send.at[1], w_recv.at[1], hd=zl * 4 + pb))
+
     for i in range(1, N_CTX):
         src = (me + i) % N_CTX
         await_recv(flag_all.at[src], flag_recv.at[src])
@@ -111,63 +165,43 @@
     slot_span = (1 - flag_sm[me, 0, 0], jnp.int32(1))
     slot_shift = (shift_of(jnp.minimum(first_rank, KEPT - 1)), shift_of(jnp.minimum(first_rank + 1, KEPT - 1)))
 
-    load_base.wait()
-    load_hidden.wait()
-
-    load_o.wait()
-    half = pl.ds(core * 256, 256)
-    other_half = pl.ds((1 - core) * 256, 256)
-    cols_a, cols_b = pl.ds(0, 2048), pl.ds(2048, 2048)
-    sends.append(send(wo.at[half, cols_a], wo_a.at[half, :], w_send.at[0], w_recv.at[0], hd=zl * 4 + pa))
-    sends.append(send(wo.at[half, cols_b], wo_b.at[half, :], w_send.at[1], w_recv.at[1], hd=zl * 4 + pb))
-
-    load_q.wait()
-    load_k.wait()
-    load_v.wait()
-
-    def project_chunk(chunk, _):
-        dx = (chunk + 1) % 4
-        targets = [ctx_at(dz, dx, dc) for dz in (1, 0) for dc in (1, 0)]
-        for slot in range(2):
-            def norm_piece(i, _):
-                target = ctx_at(1 - i // 2, dx, 1 - i % 2)
-                piece = slot_span[slot] * 16 + (target + N_CTX - slot_shift[slot]) % N_CTX
-                total = jnp.zeros((PIECE, 128), F32)
-                for c in range(0, 4096, 512):
-                    part = hidden[piece, :, c:c + 512].astype(F32)
-                    part = part * part
-                    total += (part[:, :128] + part[:, 128:256]) + (part[:, 256:384] + part[:, 384:])
-                scale = lax.rsqrt(jnp.sum(total, axis=1, keepdims=True) * (1.0 / 4096) + 1e-05)
-                dst = pl.ds(pl.multiple_of(i * 64 + slot * PIECE, PIECE), PIECE)
-                for c in range(0, 4096, 512):
-                    part = hidden[piece, :, c:c + 512].astype(F32)
-                    normed[dst, c:c + 512] = (part * scale * gain_ref[:, c:c + 512]).astype(BF16)
-                return 0
-            lax.fori_loop(0, 4, norm_piece, 0)
-        projected = jnp.dot(normed[...], wqkv[...], preferred_element_type=F32)
-        for i, target in enumerate(targets):
+    routes = (
+        (1, 2, 0), (1, 2, 1), (0, 1, 0), (0, 3, 1), (1, 1, 0), (1, 3, 1), (0, 2, 0), (0, 2, 1),
+        (1, 1, 1), (1, 3, 0), (0, 1, 1), (0, 3, 0), (1, 0, 0), (1, 0, 1), (0, 0, 1),
+    )
+
+    def spread(raw, stage, got, ssem, rsem):
+        for route in routes + ((0, 0, 0),):
+            target = ctx_at(*route)
             for slot in range(2):
                 piece = slot_span[slot] * 16 + (target + N_CTX - slot_shift[slot]) % N_CTX
-                cos_base, sin_base = base[piece, 0], base[piece, 1]
-                cosine = cos_base * inner_ref[0] - sin_base * inner_ref[1]
-                sine = sin_base * inner_ref[2] + cos_base * inner_ref[3]
-                lo = i * 64 + slot * PIECE
-                for part in range(6):
-                    block = projected[lo:lo + PIECE, part * 128:(part + 1) * 128]
-                    if part < 5:
-                        block = block * cosine + pltpu.roll(block, 64, 1) * sine
-                    stage[target, slot, part] = block.astype(BF16)
-            if i < 3:
-                send(stage.at[target], recv.at[me], a2a_send.at[target], a2a_recv.at[me], ctx=target)
+                stage[target, slot] = raw[piece]
+            if route != (0, 0, 0):
+                send(stage.at[target], got.at[me], ssem.at[target], rsem.at[me], ctx=target)
             else:
-                @pl.when(chunk < 3)
-                def _():
-                    send(stage.at[target], recv.at[me], a2a_send.at[target], a2a_recv.at[me], ctx=target)
-        return 0
-
-    lax.fori_loop(0, 4, project_chunk, 0)
-    own = pltpu.make_async_copy(stage.at[me], recv.at[me], local_sem)
-    own.start()
+                got[me] = stage[target]
+
+    def collect(got, rsem):
+        for route in routes:
+            src = ctx_at(*route)
+            await_recv(got.at[src], rsem.at[src])
+
+    spread(kv_raw, kv_stage, kv_got, kva_send, kva_recv)
+
+    load_q.wait()
+
+    def project_q(c, _):
+        rows = normed[pl.ds(c * 8, 8)].reshape(256, 4096)
+        projected = jnp.dot(rows, wq[...], preferred_element_type=F32)
+        for i in range(8):
+            rope = rope_of(c * 8 + i)
+            for part in range(4):
+                block = projected[i * PIECE:(i + 1) * PIECE, part * 128:(part + 1) * 128]
+                q_raw[c * 8 + i, part] = turned(block, rope)
+        return 0
+
+    lax.fori_loop(0, 4, project_q, 0)
+    spread(q_raw, q_stage, q_got, qa_send, qa_recv)
 
     arrival = [jnp.int32(0)] * KEPT
     rank = jnp.int32(0)
@@ -177,18 +211,14 @@
             for r in range(KEPT):
                 arrival[r] = jnp.where((flag == 1) & (rank == r), place, arrival[r])
             rank = rank + flag
-    own.wait()
-    for i in range(1, N_CTX):
-        src = (me + i) % N_CTX
-        await_recv(recv.at[src], a2a_recv.at[src])
-
+    arrival = [(place // 2, place % 2) for place in arrival]
+
+    collect(kv_got, kva_recv)
     for r in range(KEPT):
-        src, slot = arrival[r] // 2, arrival[r] % 2
-        for part in range(4):
-            queries[r * 128 + part * 32:r * 128 + part * 32 + 32, :] = recv[src, slot, part]
+        src, slot = arrival[r]
         rows = slice((r % 4) * 32, (r % 4) * 32 + 32)
-        kv[r // 4, me, 0, rows, :] = recv[src, slot, 4]
-        kv[r // 4, me, 1, rows, :] = recv[src, slot, 5]
+        kv[r // 4, me, 0, rows, :] = kv_got[src, slot, 0]
+        kv[r // 4, me, 1, rows, :] = kv_got[src, slot, 1]
 
     sibling = ctx_at(0, 0, 1)
     zmate = ctx_at(1, 0, 0)
@@ -302,30 +332,23 @@
             pl.ds(pl.multiple_of(2048 + c * width, width), width),
         )
 
-    def project_far(z):
-        await_recv(att_a.at[1, z], att_recv.at[z, 0])
-        await_recv(att_b.at[1, z], att_recv.at[z, 1])
+    def project_out(z):
+        for i in range(4):
+            await_recv(att_a.at[0, z], att_recv.at[z, i])
 
         def step(c, _):
             cols, cols_b = two_cols(c)
-            total = term(att[pb, z], wo[:, cols]) + term(att_a[1, z], wo_a[:, cols])
-            part_a[z, c] = total.astype(BF16)
-            send(part_a.at[z, c], got_a.at[z, c], part_send.at[z, 0, c], part_recv.at[z, 0, c], hd=at_pb)
-            total = term(att[pa, z], wo[:, cols_b]) + term(att_b[1, z], wo_b[:, cols])
-            part_b[z, c] = total.astype(BF16)
-            send(part_b.at[z, c], got_b.at[z, c], part_send.at[z, 1, c], part_recv.at[z, 1, c], hd=at_pa)
-            return 0
-
-        lax.fori_loop(0, steps, step, 0)
-
-    def project_near(z):
-        await_recv(att_a.at[0, z], att_recv.at[z, 2])
-        await_recv(att_b.at[0, z], att_recv.at[z, 3])
-
-        def step(c, _):
-            cols, cols_b = two_cols(c)
-            mine[z, c] = term(att[y, z], wo[:, cols]) + term(att_a[0, z], wo_a[:, cols])
-            mine[z, steps + c] = term(att[y, z], wo[:, cols_b]) + term(att_b[0, z], wo_b[:, cols])
+            sides = (
+                (0, cols, pb, att_a, wo_a, part_a, got_a, at_pb),
+                (1, cols_b, pa, att_b, wo_b, part_b, got_b, at_pa),
+            )
+            for side, own_cols, other, att_s, wo_s, part_s, got_s, hd in sides:
+                own = jnp.concatenate([att[other, z], att[y, z]], axis=0)
+                theirs = jnp.concatenate([att_s[1, z], att_s[0, z]], axis=0)
+                total = term(own, wo[:, own_cols]) + term(theirs, wo_s[:, cols])
+                part_s[z, c] = total[:64].astype(BF16)
+                send(part_s.at[z, c], got_s.at[z, c], part_send.at[z, side, c], part_recv.at[z, side, c], hd=hd)
+                mine[z, side * steps + c] = total[64:]
             return 0
 
         lax.fori_loop(0, steps, step, 0)
@@ -361,15 +384,19 @@
 
     for q in range(4):
         pass_on(q, me, 0, zmate)
+    gather_own(0)
+    gather_own(1)
     acc[...] = jnp.zeros_like(acc)
     peak[...] = jnp.full(peak.shape, -1e30, F32)
-    gather_own(0)
     gather_mate(0)
-    gather_own(1)
     gather_mate(1)
     gather_near(0)
     gather_own(2)
     gather_mate(2)
+    collect(q_got, qa_recv)
+    for r in range(KEPT):
+        src, slot = arrival[r]
+        queries[r * 128:(r + 1) * 128, :] = q_got[src, slot].reshape(128, 128)
     gather_far(0)
     gather_end(0)
 
@@ -380,8 +407,8 @@
         2: lambda: gather_near(2),
         3: lambda: (gather_end(1), weights_end()),
         4: lambda: (finish(0), finish(1), exchange(0), gather_far(2), gather_near(3)),
-        6: lambda: (gather_end(2), project_far(0)),
-        7: lambda: (finish(2), gather_far(3), project_near(0)),
+        6: lambda: (gather_end(2), project_out(0)),
+        7: lambda: (finish(2), gather_far(3)),
         8: lambda: (gather_end(3), sum_up(0)),
     }
 
@@ -405,8 +432,7 @@
     lax.fori_loop(0, len(plan), attention_step, 0)
     finish(3)
     exchange(1)
-    project_far(1)
-    project_near(1)
+    project_out(1)
     sum_up(1)
 
     own_rows = zl
@@ -430,7 +456,8 @@
 
     for i in range(1, N_CTX):
         target = (me + i) % N_CTX
-        await_send(stage.at[target], a2a_send.at[target])
+        await_send(kv_stage.at[target], kva_send.at[target])
+        await_send(q_stage.at[target], qa_send.at[target])
 
     def drain_kv(q, _):
         for way in range(4):
@@ -474,17 +501,22 @@
         out_specs=vmem,
         scratch_shapes=[
             pltpu.VMEM((32, 32, 4096), BF16),
-            pltpu.VMEM((4096, 768), BF16),
+            pltpu.VMEM((4096, 512), BF16),
+            pltpu.VMEM((4096, 256), BF16),
             pltpu.VMEM((512, 4096), BF16),
             pltpu.VMEM((512, 2048), BF16),
             pltpu.VMEM((512, 2048), BF16),
             pltpu.VMEM((32, 2, 1, 128), F32),
-            pltpu.VMEM((256, 4096), BF16),
+            pltpu.VMEM((32, 32, 4096), BF16),
             pltpu.VMEM((1, 128), jnp.int32),
             pltpu.VMEM((16, 1, 128), jnp.int32),
             pltpu.SMEM((16, 1, 128), jnp.int32),
-            pltpu.VMEM((16, 2, 6, 32, 128), BF16),
-            pltpu.VMEM((16, 2, 6, 32, 128), BF16),
+            pltpu.VMEM((32, 2, 32, 128), BF16),
+            pltpu.VMEM((32, 4, 32, 128), BF16),
+            pltpu.VMEM((16, 2, 2, 32, 128), BF16),
+            pltpu.VMEM((16, 2, 4, 32, 128), BF16),
+            pltpu.VMEM((16, 2, 2, 32, 128), BF16),
+            pltpu.VMEM((16, 2, 4, 32, 128), BF16),
             pltpu.VMEM((2048, 128), BF16),
             pltpu.VMEM((4, 16, 2, 128, 128), BF16),
             pltpu.VMEM((2048, 256), F32),
@@ -499,7 +531,9 @@
             pltpu.VMEM((2, 8, 64, 512), F32),
             pltpu.VMEM((8, 64, 512), BF16),
             pltpu.VMEM((8, 64, 512), BF16),
+            dma((4,)),
             dma((8,)),
+            dma((16,)), dma((16,)),
             dma((16,)), dma((16,)),
             dma((16,)), dma((16,)),
             dma((4, 16, 4)), dma((4, 16)),

time: 109 us -> 101 us (0.927)
  Pallas kernels: 107 us -> 99 us
    pallas_call x1, Pallas kernels: 107 us -> 99 us  [body(): pl.pallas_call(kernel, out_shape=jax.ShapeDtypeStruct((64, 4096), BF16),...]
where the time goes in v3:
time: 101 us
  Pallas kernels  99 us (98%)
  local copies, waits for them, and re-layouts  1.87 us (2%)
    pallas_call x1, Pallas kernels, body(): pl.pallas_call(kernel, out_shape=jax.ShapeDtypeStruct((64, 4096), BF16),...  99 us

profile of v3, /device:TPU:32, one launch (start us, length us, event | category | flops | bytes accessed | tf_op | source)
XLA Modules:
  0.0 100.9 jit_solution(17814520697316846513)
XLA Ops:
  0.0 99.0 %prefill.1 = bf16[64,4096]{1,0:T(8,128)(2,1)} custom-call(bf16[32,32,4096]{2,1,0:T(8,128)(2,1)} %bitcast.2, f32[1,4096]{1,0:T(1,128)} %bitcast.3, bf16[4096,512]{1,0:T(8,128)(2,1)} %wq_hbm.1, bf16[4096,128]{1,0:T(8,128)(2,1)} %wk_hbm.1, bf16[4096,128]{1,0:T(8,128)(2,1)} %wv_hbm.1, bf16[512,4096]{1,0:T(8,128)(2,1)} %wo_hbm.1, s32[2]{0:T(128)} %flags_ref.1, ...), custom_call_target="tpu_custom_call" | custom-call | tf_op jit(solution)/shard_map/prefill/pallas_call | solution.py:497
  99.0 1.9 %copy.12 = bf16[64,4096]{1,0:T(8,128)(2,1)} copy(bf16[64,4096]{1,0:T(8,128)(2,1)} %prefill.1) | data formatting | bytes 1048576

commit v4 on v3

--- a/solution.py
+++ b/solution.py
@@ -93,14 +93,6 @@
         pl.semaphore_signal(barrier, inc=1, device_id=((me + i) % N_CTX, head), device_id_type=MESH)
     for hd in (zl * 4 + pa, zl * 4 + pb, (1 - zl) * 4 + y):
         pl.semaphore_signal(barrier, inc=1, device_id=(me, hd), device_id_type=MESH)
-    pl.semaphore_wait(barrier, N_CTX - 1 + 3)
-
-    lane = lax.broadcasted_iota(jnp.int32, (1, 128), 1)
-    own_flags = jnp.where(lane == 0, flags_ref[0], jnp.where(lane == 1, flags_ref[1], 0))
-    flag_src[...] = own_flags
-    flag_all[me] = own_flags
-    for i in range(1, N_CTX):
-        sends.append(send(flag_src, flag_all.at[me], flag_send.at[i], flag_recv.at[me], ctx=(me + i) % N_CTX))
 
     load_base.wait()
     load_k.wait()
@@ -139,7 +131,18 @@
             kv_raw[c * 8 + i, 1] = block[:, 128:].astype(BF16)
         return 0
 
-    lax.fori_loop(0, 4, project_kv, 0)
+    lax.fori_loop(0, 1, project_kv, 0)
+
+    pl.semaphore_wait(barrier, N_CTX - 1 + 3)
+
+    lane = lax.broadcasted_iota(jnp.int32, (1, 128), 1)
+    own_flags = jnp.where(lane == 0, flags_ref[0], jnp.where(lane == 1, flags_ref[1], 0))
+    flag_src[...] = own_flags
+    flag_all[me] = own_flags
+    for i in range(1, N_CTX):
+        sends.append(send(flag_src, flag_all.at[me], flag_send.at[i], flag_recv.at[me], ctx=(me + i) % N_CTX))
+
+    lax.fori_loop(1, 4, project_kv, 0)
 
     load_o.wait()
     half = pl.ds(core * 256, 256)
@@ -170,23 +173,26 @@
         (1, 1, 1), (1, 3, 0), (0, 1, 1), (0, 3, 0), (1, 0, 0), (1, 0, 1), (0, 0, 1),
     )
 
-    def spread(raw, stage, got, ssem, rsem):
-        for route in routes + ((0, 0, 0),):
-            target = ctx_at(*route)
-            for slot in range(2):
-                piece = slot_span[slot] * 16 + (target + N_CTX - slot_shift[slot]) % N_CTX
-                stage[target, slot] = raw[piece]
-            if route != (0, 0, 0):
-                send(stage.at[target], got.at[me], ssem.at[target], rsem.at[me], ctx=target)
-            else:
-                got[me] = stage[target]
+    def arrange(raw, stage, route):
+        target = ctx_at(*route)
+        for slot in range(2):
+            piece = slot_span[slot] * 16 + (target + N_CTX - slot_shift[slot]) % N_CTX
+            stage[target, slot] = raw[piece]
+
+    def part_with(stage, got, ssem, rsem, route):
+        target = ctx_at(*route)
+        send(stage.at[target], got.at[me], ssem.at[target], rsem.at[me], ctx=target)
 
     def collect(got, rsem):
         for route in routes:
             src = ctx_at(*route)
             await_recv(got.at[src], rsem.at[src])
 
-    spread(kv_raw, kv_stage, kv_got, kva_send, kva_recv)
+    for route in routes:
+        arrange(kv_raw, kv_stage, route)
+        part_with(kv_stage, kv_got, kva_send, kva_recv, route)
+    arrange(kv_raw, kv_stage, (0, 0, 0))
+    kv_got[me] = kv_stage[me]
 
     load_q.wait()
 
@@ -201,7 +207,9 @@
         return 0
 
     lax.fori_loop(0, 4, project_q, 0)
-    spread(q_raw, q_stage, q_got, qa_send, qa_recv)
+    for route in routes + ((0, 0, 0),):
+        arrange(q_raw, q_stage, route)
+    q_got[me] = q_stage[me]
 
     arrival = [jnp.int32(0)] * KEPT
     rank = jnp.int32(0)
@@ -213,93 +221,105 @@
             rank = rank + flag
     arrival = [(place // 2, place % 2) for place in arrival]
 
+    def place_of(dz, dx, dc):
+        return ((x + dx) % 4) * 4 + ((zh + dz) % 2) * 2 + (core + dc) % 2
+
+    own_place = place_of(0, 0, 0)
     collect(kv_got, kva_recv)
     for r in range(KEPT):
         src, slot = arrival[r]
         rows = slice((r % 4) * 32, (r % 4) * 32 + 32)
-        kv[r // 4, me, 0, rows, :] = kv_got[src, slot, 0]
-        kv[r // 4, me, 1, rows, :] = kv_got[src, slot, 1]
+        kv[r // 4, own_place, 0, rows, :] = kv_got[src, slot, 0]
+        kv[r // 4, own_place, 1, rows, :] = kv_got[src, slot, 1]
 
     sibling = ctx_at(0, 0, 1)
     zmate = ctx_at(1, 0, 0)
     xplus, xminus = ctx_at(0, 1, 0), ctx_at(0, 3, 0)
 
     def pass_on(q, src, way, target):
-        send(kv.at[q, src], kv.at[q, src], kv_send.at[q, src, way], kv_recv.at[q, src], ctx=target)
+        place = place_of(*src)
+        send(kv.at[q, place], kv.at[q, place], kv_send.at[q, place, way], kv_recv.at[q, place], ctx=target)
 
     def arrived(q, src):
-        await_recv(kv.at[q, src], kv_recv.at[q, src])
+        place = place_of(*src)
+        await_recv(kv.at[q, place], kv_recv.at[q, place])
 
     def gather_own(q):
-        pass_on(q, me, 1, xplus)
-        pass_on(q, me, 2, xminus)
-        pass_on(q, me, 3, sibling)
+        pass_on(q, (0, 0, 0), 1, xplus)
+        pass_on(q, (0, 0, 0), 2, xminus)
+        pass_on(q, (0, 0, 0), 3, sibling)
 
     def gather_mate(q):
-        arrived(q, zmate)
-        pass_on(q, zmate, 1, xplus)
-        pass_on(q, zmate, 2, xminus)
-        pass_on(q, zmate, 3, sibling)
+        arrived(q, (1, 0, 0))
+        pass_on(q, (1, 0, 0), 1, xplus)
+        pass_on(q, (1, 0, 0), 2, xminus)
+        pass_on(q, (1, 0, 0), 3, sibling)
 
     def gather_near(q):
         for dz in range(2):
-            left, right = ctx_at(dz, 3, 0), ctx_at(dz, 1, 0)
-            arrived(q, left)
+            arrived(q, (dz, 3, 0))
             if dz == 0:
-                pass_on(q, left, 1, xplus)
-            pass_on(q, left, 3, sibling)
-            arrived(q, right)
+                pass_on(q, (dz, 3, 0), 1, xplus)
+            pass_on(q, (dz, 3, 0), 3, sibling)
+            arrived(q, (dz, 1, 0))
             if dz == 1:
-                pass_on(q, right, 2, xminus)
-            pass_on(q, right, 3, sibling)
+                pass_on(q, (dz, 1, 0), 2, xminus)
+            pass_on(q, (dz, 1, 0), 3, sibling)
 
     def gather_far(q):
         for dz in range(2):
-            across = ctx_at(dz, 2, 0)
-            arrived(q, across)
-            pass_on(q, across, 3, sibling)
-
-    def gather_end(q):
+            arrived(q, (dz, 2, 0))
+            pass_on(q, (dz, 2, 0), 3, sibling)
+
+    def gather_end(q, dx):
         for dz in range(2):
-            for dx in range(4):
-                arrived(q, ctx_at(dz, dx, 1))
+            arrived(q, (dz, dx, 1))
 
     factor = LOG2E / math.sqrt(HEAD_DIM)
     block_rows = 128
-    blocks = 512 // block_rows
-
-    def attend(g, q, masked):
-        keys = kv[q, :, 0].reshape(2048, 128)
-        values = jnp.concatenate([kv[q, :, 1].reshape(2048, 128), jnp.ones((2048, 128), BF16)], axis=1)
-        if masked:
-            key_lane = lax.broadcasted_iota(jnp.int32, (1, 2048), 1)
-            key_pos = jnp.zeros((1, 2048), jnp.int32)
-            for b in range(4):
-                place = (key_lane // 128 + N_CTX - shift_of(4 * q + b)) % N_CTX
-                here = (key_lane % 128) // 32 == b
-                key_pos = jnp.where(here, b * SPAN + place * PIECE + key_lane % PIECE, key_pos)
+
+    def attend(g, at_x):
+        sources = pl.ds(pl.multiple_of(at_x * 4, 4), 4)
 
         def rows_of(a):
-            return pl.ds(pl.multiple_of(g * 512 + a * block_rows, block_rows), block_rows)
+            return slice((4 * g + a) * block_rows, (4 * g + a + 1) * block_rows)
+
+        def keys_or_values(a, which):
+            seen = 32 * (a + 1)
+            last = kv[g, sources, which, :seen].reshape(4 * seen, 128)
+            if g == 0:
+                return last
+            return jnp.concatenate([kv[:g, sources, which].reshape(g * 512, 128), last], axis=0)
 
         def score(a):
             return lax.dot_general(
-                queries[rows_of(a), :], keys, (((1,), (1,)), ((), ())), preferred_element_type=F32
+                queries[rows_of(a), :], keys_or_values(a, 0), (((1,), (1,)), ((), ())), preferred_element_type=F32
             )
 
+        def visible(a):
+            seen = 32 * (a + 1)
+            lane = lax.broadcasted_iota(jnp.int32, (1, 4 * seen), 1)
+            source, within = lane // seen, lane % seen
+            owner = (source // 2) * 8 + at_x * 2 + source % 2
+            shift = shift_of(4 * g + a)
+            key_pos = ((owner + N_CTX - shift) % N_CTX) * PIECE + within - a * PIECE
+            key_pos = jnp.where(within < a * PIECE, -1, key_pos)
+            row = lax.broadcasted_iota(jnp.int32, (block_rows, 1), 0) % PIECE
+            return key_pos <= ((me + N_CTX - shift) % N_CTX) * PIECE + row
+
         scores = score(0)
-        for a in range(blocks):
+        for a in range(4):
             rows = rows_of(a)
-            coming = score(a + 1) if a + 1 < blocks else None
-            if masked:
-                row = lax.broadcasted_iota(jnp.int32, (block_rows, 1), 0) % PIECE
-                query_pos = a * SPAN + ((me + N_CTX - shift_of(4 * q + a)) % N_CTX) * PIECE + row
-                scores = jnp.where(key_pos <= query_pos, scores, -1e30)
+            coming = score(a + 1) if a < 3 else None
+            last = jnp.where(visible(a), scores[:, g * 512:], -1e30)
+            scores = last if g == 0 else jnp.concatenate([scores[:, :g * 512], last], axis=1)
             old = peak[rows, :]
             new = jnp.maximum(old, jnp.max(scores, axis=1, keepdims=True))
             peak[rows, :] = new
             expo = jnp.exp2((scores - new[:, :1]) * factor).astype(BF16)
             fade = jnp.exp2((old - new) * factor)
+            values = keys_or_values(a, 1)
+            values = jnp.concatenate([values, jnp.ones(values.shape, BF16)], axis=1)
             mixed = jnp.dot(expo, values, preferred_element_type=F32)
             acc[rows, :] = acc[rows, :] * jnp.concatenate([fade, fade], axis=1) + mixed
             scores = coming
@@ -332,10 +352,11 @@
             pl.ds(pl.multiple_of(2048 + c * width, width), width),
         )
 
-    def project_out(z):
+    def exchanged(z):
         for i in range(4):
             await_recv(att_a.at[0, z], att_recv.at[z, i])
 
+    def project_out(z, first, last):
         def step(c, _):
             cols, cols_b = two_cols(c)
             sides = (
@@ -351,9 +372,9 @@
                 mine[z, side * steps + c] = total[64:]
             return 0
 
-        lax.fori_loop(0, steps, step, 0)
-
-    def sum_up(z):
+        lax.fori_loop(first, last, step, 0)
+
+    def sum_up(z, first, last):
         def step(c, _):
             for side, got in ((0, got_a), (1, got_b)):
                 slot = side * steps + c
@@ -370,7 +391,7 @@
                     send(zsend.at[slot], zgot.at[slot], z_send.at[slot], z_recv.at[slot], hd=at_z)
             return 0
 
-        lax.fori_loop(0, steps, step, 0)
+        lax.fori_loop(first, last, step, 0)
 
     def weights_across():
         await_recv(wo_a.at[half, :], w_recv.at[0])
@@ -383,57 +404,57 @@
         await_recv(wo_b.at[other_half, :], wc_recv.at[1])
 
     for q in range(4):
-        pass_on(q, me, 0, zmate)
+        pass_on(q, (0, 0, 0), 0, zmate)
+    for route in routes[:8]:
+        part_with(q_stage, q_got, qa_send, qa_recv, route)
     gather_own(0)
     gather_own(1)
+    gather_own(2)
+    gather_own(3)
+    for route in routes[8:]:
+        part_with(q_stage, q_got, qa_send, qa_recv, route)
     acc[...] = jnp.zeros_like(acc)
     peak[...] = jnp.full(peak.shape, -1e30, F32)
-    gather_mate(0)
-    gather_mate(1)
-    gather_near(0)
-    gather_own(2)
-    gather_mate(2)
+    for q in range(4):
+        gather_mate(q)
     collect(q_got, qa_recv)
     for r in range(KEPT):
         src, slot = arrival[r]
         queries[r * 128:(r + 1) * 128, :] = q_got[src, slot].reshape(128, 128)
-    gather_far(0)
-    gather_end(0)
-
-    plan = ((0, 0), (1, 0), (2, 0), (3, 0), (1, 1), (2, 1), (3, 1), (2, 2), (3, 2), (3, 3))
-    after = {
-        0: lambda: (gather_near(1), weights_across()),
-        1: lambda: (gather_own(3), gather_mate(3), gather_far(1)),
-        2: lambda: gather_near(2),
-        3: lambda: (gather_end(1), weights_end()),
-        4: lambda: (finish(0), finish(1), exchange(0), gather_far(2), gather_near(3)),
-        6: lambda: (gather_end(2), project_out(0)),
-        7: lambda: (finish(2), gather_far(3)),
-        8: lambda: (gather_end(3), sum_up(0)),
-    }
-
-    def attention_step(i, _):
-        g, q = jnp.int32(0), jnp.int32(0)
-        for k, (gk, qk) in enumerate(plan):
-            g, q = jnp.where(i == k, gk, g), jnp.where(i == k, qk, q)
-
-        @pl.when(g == q)
-        def _():
-            attend(g, q, True)
-
-        @pl.when(g != q)
-        def _():
-            attend(g, q, False)
-
-        for k, work in after.items():
-            pl.when(i == k)(lambda work=work: (work(), None)[1])
-        return 0
-
-    lax.fori_loop(0, len(plan), attention_step, 0)
+    for q in range(4):
+        gather_end(q, 0)
+
+    before = {(i, g): (lambda i=i, g=g: gather_end(g, (0, 1, 3, 2)[i])) for i in range(1, 4) for g in range(4)}
+    after = {(0, g): (lambda g=g: gather_near(g)) for g in range(4)}
+    after.update({(2, g): (lambda g=g: gather_far(g)) for g in range(4)})
+    after[1, 1] = weights_across
+    after[2, 3] = lambda: (gather_far(3), weights_end())
+    after[3, 1] = lambda: (finish(0), finish(1), exchange(0))
+    after[3, 2] = lambda: finish(2)
+
+    def attention_pass(i, _):
+        at_x = (x + jnp.where(i == 3, 2, jnp.where(i == 2, 3, i))) % 4
+        for g in range(4):
+            for k in range(4):
+                if (k, g) in before:
+                    pl.when(i == k)(lambda work=before[k, g]: (work(), None)[1])
+            attend(g, at_x)
+            for k in range(4):
+                if (k, g) in after:
+                    pl.when(i == k)(lambda work=after[k, g]: (work(), None)[1])
+        return 0
+
+    lax.fori_loop(0, 4, attention_pass, 0)
     finish(3)
     exchange(1)
-    project_out(1)
-    sum_up(1)
+    turns = ((0, 0, 2), (1, 0, 1), (0, 2, 3), (1, 1, 2), (0, 3, 4), (1, 2, 4))
+    exchanged(0)
+    for k, turn in enumerate(turns):
+        if k == 1:
+            exchanged(1)
+        project_out(*turn)
+    for turn in turns:
+        sum_up(*turn)
 
     own_rows = zl
 
@@ -460,16 +481,19 @@
         await_send(q_stage.at[target], qa_send.at[target])
 
     def drain_kv(q, _):
+        def sent(src, way):
+            place = place_of(*src)
+            await_send(kv.at[q, place], kv_send.at[q, place, way])
+
         for way in range(4):
-            await_send(kv.at[q, me], kv_send.at[q, me, way])
+            sent((0, 0, 0), way)
         for way in range(1, 4):
-            await_send(kv.at[q, zmate], kv_send.at[q, zmate, way])
+            sent((1, 0, 0), way)
         for dz in range(2):
             for dx in range(1, 4):
-                src = ctx_at(dz, dx, 0)
-                await_send(kv.at[q, src], kv_send.at[q, src, 3])
-        await_send(kv.at[q, ctx_at(0, 3, 0)], kv_send.at[q, ctx_at(0, 3, 0), 1])
-        await_send(kv.at[q, ctx_at(1, 1, 0)], kv_send.at[q, ctx_at(1, 1, 0), 2])
+                sent((dz, dx, 0), 3)
+        sent((0, 3, 0), 1)
+        sent((1, 1, 0), 2)
         return 0
 
     lax.fori_loop(0, 4, drain_kv, 0)

time: 101 us -> 97.4 us (0.964)
  Pallas kernels: 99 us -> 94.8 us
    pallas_call x1, Pallas kernels: 99 us -> 94.8 us  [body(): pl.pallas_call(kernel, out_shape=jax.ShapeDtypeStruct((64, 4096), BF16),...]
where the time goes in v4:
time: 97.4 us; the launch traced here: 96.7 us
  Pallas kernels  94.8 us (97%)
  local copies, waits for them, and re-layouts  1.87 us (2%)
    pallas_call x1, Pallas kernels, body(): pl.pallas_call(kernel, out_shape=jax.ShapeDtypeStruct((64, 4096), BF16),...  94.8 us

profile of v4, /device:TPU:32, one launch (start us, length us, event | category | flops | bytes accessed | tf_op | source)
XLA Modules:
  0.0 96.7 jit_solution(10128927467896067566)
XLA Ops:
  0.0 94.8 %prefill.1 = bf16[64,4096]{1,0:T(8,128)(2,1)} custom-call(bf16[32,32,4096]{2,1,0:T(8,128)(2,1)} %bitcast.2, f32[1,4096]{1,0:T(1,128)} %bitcast.3, bf16[4096,512]{1,0:T(8,128)(2,1)} %wq_hbm.1, bf16[4096,128]{1,0:T(8,128)(2,1)} %wk_hbm.1, bf16[4096,128]{1,0:T(8,128)(2,1)} %wv_hbm.1, bf16[512,4096]{1,0:T(8,128)(2,1)} %wo_hbm.1, s32[2]{0:T(128)} %flags_ref.1, ...), custom_call_target="tpu_custom_call" | custom-call | tf_op jit(solution)/shard_map/prefill/pallas_call | solution.py:521
  94.8 1.9 %copy.12 = bf16[64,4096]{1,0:T(8,128)(2,1)} copy(bf16[64,4096]{1,0:T(8,128)(2,1)} %prefill.1) | data formatting | bytes 1048576

commit v5 on v4

--- a/solution.py
+++ b/solution.py
@@ -425,7 +425,11 @@
         gather_end(q, 0)
 
     before = {(i, g): (lambda i=i, g=g: gather_end(g, (0, 1, 3, 2)[i])) for i in range(1, 4) for g in range(4)}
-    after = {(0, g): (lambda g=g: gather_near(g)) for g in range(4)}
+    after = {
+        (0, 1): lambda: gather_near(0),
+        (0, 2): lambda: gather_near(1),
+        (0, 3): lambda: (gather_near(2), gather_near(3)),
+    }
     after.update({(2, g): (lambda g=g: gather_far(g)) for g in range(4)})
     after[1, 1] = weights_across
     after[2, 3] = lambda: (gather_far(3), weights_end())

time: 97.4 us -> 97.3 us (level)
  no operation moved by 1% of the time
where the time goes in v5:
time: 97.3 us; the launch traced here: 96.3 us
  Pallas kernels  94.5 us (97%)
  local copies, waits for them, and re-layouts  1.87 us (2%)
    pallas_call x1, Pallas kernels, body(): pl.pallas_call(kernel, out_shape=jax.ShapeDtypeStruct((64, 4096), BF16),...  94.5 us

profile of v5, /device:TPU:32, one launch (start us, length us, event | category | flops | bytes accessed | tf_op | source)
XLA Modules:
  0.0 96.3 jit_solution(15919292444116335561)
XLA Ops:
  0.0 94.5 %prefill.1 = bf16[64,4096]{1,0:T(8,128)(2,1)} custom-call(bf16[32,32,4096]{2,1,0:T(8,128)(2,1)} %bitcast.2, f32[1,4096]{1,0:T(1,128)} %bitcast.3, bf16[4096,512]{1,0:T(8,128)(2,1)} %wq_hbm.1, bf16[4096,128]{1,0:T(8,128)(2,1)} %wk_hbm.1, bf16[4096,128]{1,0:T(8,128)(2,1)} %wv_hbm.1, bf16[512,4096]{1,0:T(8,128)(2,1)} %wo_hbm.1, s32[2]{0:T(128)} %flags_ref.1, ...), custom_call_target="tpu_custom_call" | custom-call | tf_op jit(solution)/shard_map/prefill/pallas_call | solution.py:525
  94.5 1.9 %copy.12 = bf16[64,4096]{1,0:T(8,128)(2,1)} copy(bf16[64,4096]{1,0:T(8,128)(2,1)} %prefill.1) | data formatting | bytes 1048576
